TPU v7x, 128 devices: a whole 4x4x4 slice. The times are simulated.
128 devices in a mesh: gx: 16 (over z_hi, x, core), gy: 8 (over y, z_lo).
Axes of the slice: x: 4, y: 4, z: 4 (z_hi: 2, z_lo: 2; z = z_hi * 2 + z_lo), core: 2. Of those that a mesh axis runs over, the one named last changes fastest.
Arguments:
- populations: float32 [19, 64, 256, 128], P(None, 'gx', 'gy'), may hold values from 0.02 to 0.09
- marker_weights: bfloat16 [6144, 64, 128], P(('gx', 'gy')), may hold values from 0 to 0.03125
- marker_force: bfloat16 [6144, 3, 128], P(('gx', 'gy')), may hold values from -0.59765625 to 0.59765625
- owner_device: int32 [6144, 1], P(('gx', 'gy')), may hold values from 0 to 127; in each aligned block of 48 rows (0 to 47, 48 to 95, ...) at most 2 rows name the same one
- stencil_base: int32 [6144, 3], P(('gx', 'gy')), may hold values from 0 to 124, as said below
- block_swimmer: int32 [6144], P(('gx', 'gy')), may hold values from 0 to 511, as said below
Outputs:
- new_populations: float32 [19, 64, 256, 128], P(None, 'gx', 'gy')
- marker_velocity: float32 [6144, 3, 128], P(('gx', 'gy'))
- swimmer_velocity: float32 [3, 512], P(None, ('gx', 'gy'))
Inputs may be any that keep to these rules, and one draw needn't show every extreme that they name: `owner_device`: among the blocks held by one device (aligned runs of 48 rows), no device is named more than 2 times, and some device is named exactly 2 times. `stencil_base`: component 0 lies in 0 to 0, component 1 in 0 to 28, component 2 in 0 to 124; each bound is taken by some block. `block_swimmer`: the blocks held by device d (gx slowest) belong to swimmers d * 4 to d * 4 + 3, and every swimmer has a block.
All inputs are finite; a program needn't handle non-finite values.
Results may differ from a plain program's by a relative error of at most 0.00056.
Values may be sent and summed in bfloat16 or wider, within the bound.
A program may use at most 64 MiB of HBM per device.

v0:
```python
import jax
import jax.numpy as jnp
import numpy as np
from jax import lax
from jax.sharding import PartitionSpec as P

STEN = 4
SWIM_DEV = 4


velocities = np.array(
    [
        [0, 0, 0],
        [1, 0, 0],
        [-1, 0, 0],
        [0, 1, 0],
        [0, -1, 0],
        [0, 0, 1],
        [0, 0, -1],
        [1, 1, 0],
        [-1, -1, 0],
        [1, -1, 0],
        [-1, 1, 0],
        [1, 0, 1],
        [-1, 0, -1],
        [1, 0, -1],
        [-1, 0, 1],
        [0, 1, 1],
        [0, -1, -1],
        [0, 1, -1],
        [0, -1, 1],
    ]
)
opposite = [0, 2, 1, 4, 3, 6, 5, 8, 7, 10, 9, 12, 11, 14, 13, 16, 15, 18, 17]
lattice_weights = np.array([1.0 / 3.0] + [1.0 / 18.0] * 6 + [1.0 / 36.0] * 12)
relax_time = 0.8
speed_scale = 20.0


def side_by_side(arrays, axis, split_dim, concat_dim, along):
    columns = [a.reshape(*a.shape[:along], -1) for a in arrays]
    both = jnp.concatenate(columns, axis=along)
    result, at, finished = (
        lax.all_to_all(both, axis, split_axis=split_dim, concat_axis=concat_dim, tiled=True),
        0,
        [],
    )
    for a, column in zip(arrays, columns):
        piece = result[..., at : at + column.shape[along]]
        finished.append(piece.reshape(*piece.shape[:along], *a.shape[along:]))
        at += column.shape[along]
    return tuple(finished)


def with_halo(block, sides, width):
    for axis, dim in sides:
        count = lax.axis_size(axis)
        forward = [(i, i + 1) for i in range(count - 1)]
        forward.append((count - 1, 0))
        backward = [(target, source) for source, target in forward]
        low = lax.ppermute(
            lax.slice_in_dim(block, block.shape[dim] - width, None, axis=dim), axis, forward
        )
        high = lax.ppermute(lax.slice_in_dim(block, 0, width, axis=dim), axis, backward)
        block = jnp.concatenate([low, block, high], axis=dim)
    return block


def signed_total(stack, component):
    plus_list = [i for i in range(19) if velocities[i, component] == 1]
    minus_list = [i for i in range(19) if velocities[i, component] == -1]
    return jnp.sum(stack[np.array(plus_list)], axis=0) - jnp.sum(
        stack[np.array(minus_list)], axis=0
    )


def moments(fields):
    density = jnp.sum(fields, axis=0)
    momentum = jnp.stack([signed_total(fields, k) for k in range(3)])
    return (density, momentum)


def collide(fields, forcing):
    density, momentum = moments(fields)
    velocity = (momentum + relax_time * forcing) / density
    project_list = []
    for direction in range(19):
        term = jnp.zeros_like(density)
        for k in range(3):
            sign = int(velocities[direction, k])
            if sign == 1:
                term = term + velocity[k]
            elif sign == -1:
                term = term - velocity[k]
        project_list.append(term)
    project = jnp.stack(project_list)
    square = jnp.sum(velocity * velocity, axis=0)
    weights = jnp.asarray(lattice_weights, jnp.float32)[:, None, None, None]
    equilibrium = weights * density * (1.0 + 3.0 * project + 4.5 * project * project - 1.5 * square)
    return fields - (fields - equilibrium) / relax_time


def stream(padded, first_row, total_rows):
    slab_cells = padded.shape[1] - 2
    strip_cells = padded.shape[2] - 2
    height = padded.shape[3]
    global_rows = first_row + jnp.arange(strip_cells, dtype=jnp.int32)
    column_cells = jnp.arange(height, dtype=jnp.int32)
    result = []
    for direction in range(19):
        move_east = int(velocities[direction, 0])
        move_north = int(velocities[direction, 1])
        move_up = int(velocities[direction, 2])
        source = padded[
            direction,
            1 - move_east : 1 - move_east + slab_cells,
            1 - move_north : 1 - move_north + strip_cells,
            :,
        ]
        source = jnp.roll(source, move_up, axis=2)
        bounce = padded[opposite[direction], 1 : 1 + slab_cells, 1 : 1 + strip_cells, :]
        anchor_row = global_rows - move_north
        anchor_cell = column_cells - move_up
        outside = ((anchor_row < 0) | (anchor_row >= total_rows))[:, None] | (
            (anchor_cell < 0) | (anchor_cell >= height)
        )[None, :]
        result.append(jnp.where(outside[None], bounce, source))
    return jnp.stack(result)


def fluid_speed(fields, forcing):
    density, momentum = moments(fields)
    return (momentum + 0.5 * forcing) / density


def body(populations, marker_weights, marker_force, owner_device, stencil_base, block_swimmer):
    slab_cells = populations.shape[1]
    strip_cells = populations.shape[2]
    height = populations.shape[3]
    cycle_size = lax.axis_size("gx")
    strip_count = lax.axis_size("gy")
    devices = cycle_size * strip_count
    held_count = marker_weights.shape[0]
    capacity = max(2, (2 * held_count + devices - 1) // devices)
    slot_count = devices * capacity
    cube_cells = STEN * STEN * STEN
    targets = owner_device[:, 0]
    block_order = jnp.arange(held_count, dtype=jnp.int32)
    earlier = (targets[:, None] == targets[None, :]) & (block_order[None, :] < block_order[:, None])
    ranking = jnp.sum(earlier.astype(jnp.int32), axis=1)
    position = targets * capacity + ranking
    placed_base = (
        jnp.zeros((slot_count, 3), jnp.float32).at[position].set(stencil_base.astype(jnp.float32))
    )
    patches = jnp.einsum(
        "bcm,bkm->bkc", marker_weights, marker_force, preferred_element_type=jnp.float32
    )
    outgoing = jnp.zeros((slot_count, 3, cube_cells), jnp.float32).at[position].set(patches)
    got_patch, got_base = side_by_side((outgoing, placed_base), ("gx", "gy"), 0, 0, 2)
    corner = got_base.astype(jnp.int32)
    anchor_zero = jnp.zeros((), jnp.int32)

    def place_patch(force_grid, slot_item):
        patch, corner_row = slot_item
        start = (anchor_zero, corner_row[0], corner_row[1], corner_row[2])
        existing = lax.dynamic_slice(force_grid, start, (3, STEN, STEN, STEN))
        return (
            lax.dynamic_update_slice(
                force_grid, existing + patch.reshape(3, STEN, STEN, STEN), start
            ),
            None,
        )

    forcing, _ = lax.scan(
        place_patch,
        jnp.zeros((3, slab_cells, strip_cells, height), jnp.float32),
        (got_patch, corner),
    )
    first_row = lax.axis_index("gy") * strip_cells
    total_rows = strip_count * strip_cells
    fields = populations
    for substep in range(2):
        relaxed = collide(fields, forcing)
        padded = with_halo(relaxed, (("gx", 1), ("gy", 2)), 1)
        fields = stream(padded, first_row, total_rows)
    velocity_field = fluid_speed(fields, forcing)

    def sample_cube(corner_row):
        start = (anchor_zero, corner_row[0], corner_row[1], corner_row[2])
        return lax.dynamic_slice(velocity_field, start, (3, STEN, STEN, STEN)).reshape(
            3, cube_cells
        )

    gathered_speed = jax.vmap(sample_cube)(corner)
    returned = lax.all_to_all(
        gathered_speed.astype(jnp.bfloat16), ("gx", "gy"), split_axis=0, concat_axis=0, tiled=True
    ).astype(gathered_speed.dtype)
    own_cells = jnp.take(returned, position, axis=0).astype(jnp.bfloat16)
    marker_velocity = speed_scale * jnp.einsum(
        "bcm,bkc->bkm", marker_weights, own_cells, preferred_element_type=jnp.float32
    )
    block_mean = jnp.mean(marker_velocity, axis=2)
    local_slot = block_swimmer % SWIM_DEV
    membership = (local_slot[:, None] == jnp.arange(SWIM_DEV, dtype=jnp.int32)[None, :]).astype(
        jnp.float32
    )
    swimmer_velocity = jnp.einsum(
        "bk,bs->ks", block_mean, membership, precision=lax.Precision.HIGHEST
    )
    return (fields, marker_velocity, swimmer_velocity)


def solution(mesh):
    in_specs = (
        P(None, "gx", "gy", None),
        P(("gx", "gy"), None, None),
        P(("gx", "gy"), None, None),
        P(("gx", "gy"), None),
        P(("gx", "gy"), None),
        P(("gx", "gy")),
    )
    out_specs = (P(None, "gx", "gy", None), P(("gx", "gy"), None, None), P(None, ("gx", "gy")))
    return jax.shard_map(body, mesh=mesh, in_specs=in_specs, out_specs=out_specs, check_vma=False)
```

profile of v0, /device:TPU:1, one launch (start us, length us, event | category | flops | bytes accessed | tf_op | source)
XLA Modules:
  0.0 2282.9 jit_solution(9274043049289235349)
XLA Ops:
  13.1 11.5 all-to-all-start
  37.9 1719.4 %while.10 = (s32[]{:T(128)}, f32[3,4,32,128]{3,2,1,0:T(8,128)S(1)}, s32[256,3]{0,1:T(4,128)S(1)}, f32[256,3,64]{2,1,0:T(4,128)S(1)}, s32[]{:T(128)}, /*index=5*/s32[]{:T(128)}, s32[]{:T(128)}, s32[]{:T(128)}) while((s32[]{:T(128)}, f32[3,4,32,128]{3,2,1,0:T(8,128)S(1)}, s32[256,3]{0,1:T(4,128)S(1)}, f32[256,3,64]{2,1,0:T(4,128)S(1)}, ...), condition=%wide.region_11.12_spmd, body=%wide.region_10.11_spmd.sunk | while | flops 200 | bytes 7125 | solution.py:174
  42.4 3.9 dynamic_update_slice.5
  55.9 3.9 dynamic_update_slice.5
  82.8 3.9 dynamic_update_slice.5
  109.6 3.9 dynamic_update_slice.5
  163.4 3.9 dynamic_update_slice.5
  176.8 3.9 dynamic_update_slice.5
  203.7 3.9 dynamic_update_slice.5
  217.2 3.9 dynamic_update_slice.5
  230.7 3.9 dynamic_update_slice.5
  244.1 3.9 dynamic_update_slice.5
  271.1 3.9 dynamic_update_slice.5
  284.5 3.9 dynamic_update_slice.5
  298.0 3.9 dynamic_update_slice.5
  324.9 3.9 dynamic_update_slice.5
  338.4 3.9 dynamic_update_slice.5
  365.3 3.9 dynamic_update_slice.5
  378.7 3.9 dynamic_update_slice.5
  405.6 3.9 dynamic_update_slice.5
  446.0 3.9 dynamic_update_slice.5
  472.9 3.9 dynamic_update_slice.5
  486.4 3.9 dynamic_update_slice.5
  526.7 3.9 dynamic_update_slice.5
  580.6 3.9 dynamic_update_slice.5
  607.5 3.9 dynamic_update_slice.5
  634.4 3.9 dynamic_update_slice.5
  647.9 3.9 dynamic_update_slice.5
  661.4 3.9 dynamic_update_slice.5
  715.2 3.9 dynamic_update_slice.5
  742.1 3.9 dynamic_update_slice.5
  755.5 3.9 dynamic_update_slice.5
  769.0 3.9 dynamic_update_slice.5
  782.5 3.9 dynamic_update_slice.5
  795.9 3.9 dynamic_update_slice.5
  903.6 3.9 dynamic_update_slice.5
  917.1 3.9 dynamic_update_slice.5
  930.5 3.9 dynamic_update_slice.5
  944.0 3.9 dynamic_update_slice.5
  957.5 3.9 dynamic_update_slice.5
  1075.4 3.9 dynamic_update_slice.5
  1102.3 3.9 dynamic_update_slice.5
  1142.7 3.9 dynamic_update_slice.5
  1209.9 3.9 dynamic_update_slice.5
  1223.4 3.9 dynamic_update_slice.5
  1263.8 3.9 dynamic_update_slice.5
  1277.2 3.9 dynamic_update_slice.5
  1290.7 3.9 dynamic_update_slice.5
  1358.0 3.9 dynamic_update_slice.5
  1384.9 3.9 dynamic_update_slice.5
  1425.3 3.9 dynamic_update_slice.5
  1492.6 3.9 dynamic_update_slice.5
  1613.8 3.9 dynamic_update_slice.5
  1640.7 3.9 dynamic_update_slice.5
  1667.6 3.9 dynamic_update_slice.5
  1681.1 3.9 dynamic_update_slice.5
  1707.9 3.9 dynamic_update_slice.5
  1721.4 3.9 dynamic_update_slice.5
  1777.9 414.9 %collective-permute-start.3 = (f32[19,6,1,128]{3,2,1,0:T(1,128)S(1)}, f32[19,6,1,128]{3,2,1,0:T(1,128)S(1)}, u32[]{:S(2)}, u32[]{:S(2)}) collective-permute-start(f32[19,6,1,128]{3,2,1,0:T(1,128)S(1)} %get-tuple-element.127), channel_id=1, source_target_pairs={{1,0},{2,1},{3,2},{4,3},{5,4},{6,5},{7,6},{0,7},{9,8},{10,9},{11,1... | collective-permute-start | bytes 175112 | tf_op jit(solution)/shard_map/ppermute | solution.py:64
  2220.8 4.0 collective-permute-start.7
  2239.3 9.4 gather_fusion.18
  2248.7 6.2 copy.292
  2255.9 14.5 all-to-all-start.1
  2270.4 9.8 all-to-all-done.1
  (1796 shorter events, 649.2 us)
Async XLA Ops:
  0.6 5.3 copy-start
  2.8 6.5 copy-start.25
  9.3 18.2 copy-start.1
  10.4 17.1 copy-start.39
  10.4 17.1 copy-start.40
  13.1 22.1 all-to-all-start
  27.6 1.9 copy-start.37
  27.6 1.9 copy-start.38
  27.6 0.6 copy-start.19
  27.6 1.2 copy-start.20
  29.4 1.9 copy-start.35
  29.4 1.9 copy-start.36
  29.5 0.6 copy-start.22
  29.5 1.2 copy-start.21
  31.3 0.6 copy-start.24
  31.4 1.2 copy-start.23
  1761.2 7.7 copy-start.28
  1770.7 0.7 copy-start.30
  1770.7 0.7 copy-start.31
  1770.7 0.7 copy-start.32
  1770.7 0.7 copy-start.33
  1770.7 0.7 copy-start.34
  1770.8 3.9 collective-permute-start
  1770.8 6.4 collective-permute-start.1
  1771.5 423.3 %copy-start.7 = (pred[32,128]{1,0:T(8,128)(4,1)}, pred[32,128]{1,0:T(8,128)(4,1)S(1)}, u32[]{:S(2)}) copy-start(pred[32,128]{1,0:T(8,128)(4,1)S(1)} %get-tuple-element.157) | copy-start | bytes 12292
  1771.5 423.3 %copy-start.9 = (pred[32,128]{1,0:T(8,128)(4,1)}, pred[32,128]{1,0:T(8,128)(4,1)S(1)}, u32[]{:S(2)}) copy-start(pred[32,128]{1,0:T(8,128)(4,1)S(1)} %get-tuple-element.158) | copy-start | bytes 12292
  1771.5 423.3 %copy-start.11 = (pred[32,128]{1,0:T(8,128)(4,1)}, pred[32,128]{1,0:T(8,128)(4,1)S(1)}, u32[]{:S(2)}) copy-start(pred[32,128]{1,0:T(8,128)(4,1)S(1)} %get-tuple-element.159) | copy-start | bytes 12292
  1771.5 423.3 %copy-start.13 = (pred[32,128]{1,0:T(8,128)(4,1)}, pred[32,128]{1,0:T(8,128)(4,1)S(1)}, u32[]{:S(2)}) copy-start(pred[32,128]{1,0:T(8,128)(4,1)S(1)} %get-tuple-element.160) | copy-start | bytes 12292
  1771.5 423.3 %copy-start.15 = (pred[32,128]{1,0:T(8,128)(4,1)}, pred[32,128]{1,0:T(8,128)(4,1)S(1)}, u32[]{:S(2)}) copy-start(pred[32,128]{1,0:T(8,128)(4,1)S(1)} %get-tuple-element.161) | copy-start | bytes 12292
  1771.5 423.3 %copy-start.17 = (pred[32,128]{1,0:T(8,128)(4,1)}, pred[32,128]{1,0:T(8,128)(4,1)S(1)}, u32[]{:S(2)}) copy-start(pred[32,128]{1,0:T(8,128)(4,1)S(1)} %get-tuple-element.162) | copy-start | bytes 12292
  1777.8 416.5 %collective-permute-start.2 = (f32[19,6,1,128]{3,2,1,0:T(1,128)S(1)}, f32[19,6,1,128]{3,2,1,0:T(1,128)S(1)}, u32[]{:S(2)}, u32[]{:S(2)}) collective-permute-start(f32[19,6,1,128]{3,2,1,0:T(1,128)S(1)} %get-tuple-element.126), channel_id=1, source_target_pairs={{0,1},{1,2},{2,3},{3,4},{4,5},{5,6},{6,7},{7,0},{8,9},{9,10},{10,1... | collective-permute-start | bytes 175112 | tf_op jit(solution)/shard_map/ppermute | solution.py:61
  1777.9 416.4 %collective-permute-start.3 = (f32[19,6,1,128]{3,2,1,0:T(1,128)S(1)}, f32[19,6,1,128]{3,2,1,0:T(1,128)S(1)}, u32[]{:S(2)}, u32[]{:S(2)}) collective-permute-start(f32[19,6,1,128]{3,2,1,0:T(1,128)S(1)} %get-tuple-element.127), channel_id=1, source_target_pairs={{1,0},{2,1},{3,2},{4,3},{5,4},{6,5},{7,6},{0,7},{9,8},{10,9},{11,1... | collective-permute-start | bytes 175112 | tf_op jit(solution)/shard_map/ppermute | solution.py:64
  2203.7 7.7 copy-start.3
  2211.5 0.7 copy-start.29
  2212.6 0.9 copy-start.41
  2212.7 4.7 collective-permute-start.4
  2213.6 6.6 collective-permute-start.5
  2220.8 5.6 collective-permute-start.6
  2220.8 6.2 collective-permute-start.7
  2224.9 2.5 copy-start.8
  2224.9 2.5 copy-start.10
  2224.9 2.5 copy-start.12
  2225.0 2.5 copy-start.14
  2225.0 2.5 copy-start.16
  2225.0 2.5 copy-start.18
  2228.8 4.9 copy-start.2
  2234.5 1.0 copy-start.4
  2234.5 1.1 copy-start.5
  2234.5 1.1 copy-start.6
  2248.6 21.7 copy-start.26
  2254.8 26.2 %copy-start.27 = (pred[48]{0:T(512)(128)(4,1)S(1)}, pred[48]{0:T(512)(128)(4,1)}, u32[]{:S(2)}) copy-start(pred[48]{0:T(512)(128)(4,1)} %get-tuple-element.66) | copy-start | bytes 148
  2254.9 27.3 %copy-start.42 = (s32[48]{0:T(128)S(1)}, s32[48]{0:T(128)}, u32[]{:S(2)}) copy-start(s32[48]{0:T(128)} %and_select_fusion) | copy-start | bytes 580
  2255.9 24.3 %all-to-all-start.1 = ((bf16[128,2,192]{2,1,0:T(2,128)(2,1)}), bf16[128,2,192]{2,1,0:T(2,128)(2,1)S(1)}, u32[]{:S(2)}, u32[]{:S(2)}) async-start(bf16[128,2,192]{2,1,0:T(2,128)(2,1)} %reshape.763), calls=%async_computation.1 | async-start | bytes 262144 | tf_op jit(solution)/shard_map/all_to_all | solution.py:195
where the time goes:
time: 2300 us; the launch traced here: 2280 us
  loops' own time  945 us (41%)
  local copies, waits for them, and re-layouts  805 us (35%)
  starting transfers between devices  446 us (19%)
  other arithmetic  55.1 us (2%)
  waiting for transfers between devices  27 us (1%)
    another operation x1, loops' own time, body(): lax.scan(place_patch, jnp.zeros((3, slab_cells, strip_cells, height), jnp...  945 us
    dynamic_update_slice x256, local copies, waits for them, and re-layouts, place_patch(): lax.dynamic_update_slice(force_grid, existing + patch.reshape(3, STEN, ST...  572 us
    ppermute x4, starting transfers between devices, with_halo(): lax.ppermute(lax.slice_in_dim(block, 0, width, axis=dim), axis, backward)  419 us
    slice x256, local copies, waits for them, and re-layouts, place_patch(): start = (anchor_zero, corner_row[0], corner_row[1], corner_row[2])  133 us
  transfers between devices with their start and end apart: 10, of which 9 were waited for; matrix products, arithmetic and copies ran while one was open for 0% of the time, Pallas kernels for 0%

commit v1 on v0

v1 whole, which is shorter than its diff:
```python
import jax
import jax.numpy as jnp
from jax import lax
from jax.experimental import pallas as pl
from jax.experimental.pallas import tpu as pltpu
from jax.sharding import PartitionSpec as P

MESH = pl.DeviceIdType.MESH
F32 = jnp.float32
BF16 = jnp.bfloat16

NGX, NGY, NDEV = 16, 8, 128
CX, CY, NZ = 4, 32, 128
HELD = 48
TOP = 8

VEL = (
    (0, 0, 0),
    (1, 0, 0), (-1, 0, 0), (0, 1, 0), (0, -1, 0), (0, 0, 1), (0, 0, -1),
    (1, 1, 0), (-1, -1, 0), (1, -1, 0), (-1, 1, 0),
    (1, 0, 1), (-1, 0, -1), (1, 0, -1), (-1, 0, 1),
    (0, 1, 1), (0, -1, -1), (0, 1, -1), (0, -1, 1),
)
OPP = (0, 2, 1, 4, 3, 6, 5, 8, 7, 10, 9, 12, 11, 14, 13, 16, 15, 18, 17)
WEIGHT = (1.0 / 3.0,) + (1.0 / 18.0,) * 6 + (1.0 / 36.0,) * 12
PAIRS = ((1, 2), (3, 4), (5, 6), (7, 8), (9, 10), (11, 12), (13, 14), (15, 16), (17, 18))

XP = (1, 7, 9, 11, 13)
XM = (2, 8, 10, 12, 14)
REST = (0, 3, 4, 5, 6, 15, 16, 17, 18)
ORDER = XP + XM + REST
AT = {d: i for i, d in enumerate(ORDER)}
YP = (3, 7, 10, 15, 17)
YM = (4, 8, 9, 16, 18)


def iota(shape, dim):
    return lax.broadcasted_iota(jnp.int32, shape, dim)


def dot(a, b):
    return jnp.dot(a, b, preferred_element_type=F32)


def dot_nt(a, b):
    return lax.dot_general(a, b, (((1,), (1,)), ((), ())), preferred_element_type=F32)


def moments(f):
    rho = f[0]
    mom = [None, None, None]
    for p, m in PAIRS:
        rho = rho + (f[p] + f[m])
        diff = f[p] - f[m]
        for k in range(3):
            if VEL[p][k] == 1:
                mom[k] = diff if mom[k] is None else mom[k] + diff
            elif VEL[p][k] == -1:
                mom[k] = mom[k] - diff
    return rho, mom


def collide(f, force):
    rho, mom = moments(f)
    inv = 1.0 / rho
    u = [(mom[k] + 0.8 * force[k]) * inv for k in range(3)]
    usq = u[0] * u[0] + u[1] * u[1] + u[2] * u[2]
    whole = 1.25 * rho
    calm = 1.0 - 1.5 * usq
    out = [None] * 19
    out[0] = (WEIGHT[0] * whole) * calm - 0.25 * f[0]
    for first, last, w in ((0, 3, 1.0 / 18.0), (3, 9, 1.0 / 36.0)):
        scaled = w * whole
        base = scaled * calm
        linear = 3.0 * scaled
        for p, m in PAIRS[first:last]:
            along = None
            for k in range(3):
                if VEL[p][k] == 1:
                    along = u[k] if along is None else along + u[k]
                elif VEL[p][k] == -1:
                    along = along - u[k]
            turn = linear * along
            even = base + 1.5 * (turn * along)
            out[p] = (even + turn) - 0.25 * f[p]
            out[m] = (even - turn) - 0.25 * f[m]
    return out


def kernel(
    pop, weights, force, owner, base, swimmer,
    new_pop, speed_out, swim_out,
    sendbuf, recvbuf, backbuf, finbuf, turned, spread_hi, spread_lo, onehot_z, forcing, pad1, pad2, fluid, sampled, samples,
    ysend, yrecv, csend, crecv,
    send_sem, recv_sem, halo_send, halo_recv,
):
    gx, gy = lax.axis_index("gx"), lax.axis_index("gy")
    me = gx * NGY + gy

    barrier = pltpu.get_barrier_semaphore()

    def greet(i, _):
        t = lax.rem(me + i, NDEV)
        pl.semaphore_signal(barrier, inc=1, device_id=(t // NGY, lax.rem(t, NGY)), device_id_type=MESH)
        return 0

    lax.fori_loop(1, NDEV, greet, 0)

    col = owner[...]
    square = (HELD, HELD)
    down, across = iota(square, 0), iota(square, 1)
    row = jnp.sum(jnp.where(down == across, col, 0), axis=0, keepdims=True)
    same = col == row
    rank_col = jnp.sum(jnp.where(same & (across < down), 1, 0), axis=1, keepdims=True)
    rank_row = jnp.sum(jnp.where(same & (down < across), 1, 0), axis=0, keepdims=True)
    slot_row = rank_row * NDEV + row
    slot_col = rank_col * NDEV + col

    lane = iota((8, 128), 1)
    left = lane < 64
    ownpart = iota((8, 512), 1) // 64 == iota((8, 512), 0)
    pulls = force[...].astype(F32)
    pulls = [pulls[:, k, :] for k in range(3)]
    corner = base[...].astype(F32)
    rows01, rows2x = [], []
    for g in range(6):
        at = slice(8 * g, 8 * g + 8)
        lhs = jnp.concatenate([pulls[k][at] for k in range(3)], axis=0).astype(BF16)
        full = dot_nt(lhs, weights[512 * g : 512 * g + 512, :])
        part = []
        for k in range(3):
            x = jnp.where(ownpart, full[8 * k : 8 * k + 8], 0.0)
            y = (x[:, 0:128] + x[:, 128:256]) + (x[:, 256:384] + x[:, 384:512])
            part.append(y + pltpu.roll(y, 64, 1))
        extra = jnp.where(lane == 64, corner[at, 1:2], jnp.where(lane == 65, corner[at, 2:3], 0.0))
        rows01.append(jnp.where(left, part[0], part[1]))
        rows2x.append(jnp.where(left, part[2], extra))
    patch = jnp.concatenate([jnp.concatenate(rows01, axis=0), jnp.concatenate(rows2x, axis=0)], axis=1)
    patch_hi = patch.astype(BF16)
    patch_lo = (patch - patch_hi.astype(F32)).astype(BF16)
    put = jnp.where(iota((256, HELD), 0) == slot_row, 1.0, 0.0).astype(BF16)
    outgoing = dot(put, patch_hi) + dot(put, patch_lo)
    for j in range(2):
        for h in range(2):
            sendbuf[:, 2 * j + h, :] = outgoing[128 * j : 128 * j + 128, 128 * h : 128 * h + 128]

    pl.semaphore_wait(barrier, NDEV - 1)

    def exchange(source, target, n):
        def send(i, _):
            t = lax.rem(me + i, NDEV)
            pltpu.make_async_remote_copy(
                source.at[t], target.at[me], send_sem.at[n], recv_sem.at[n],
                device_id=(t // NGY, lax.rem(t, NGY)), device_id_type=MESH,
            ).start()
            return 0

        lax.fori_loop(1, NDEV, send, 0)
        target[me] = source[me]

    def exchanged(source, target, n):
        pltpu.make_async_remote_copy(
            source.at[pl.ds(0, NDEV - 1)], target.at[pl.ds(0, NDEV - 1)], send_sem.at[n], recv_sem.at[n],
            device_id=(lax.rem(gx + 1, NGX), gy), device_id_type=MESH,
        ).wait()

    exchange(sendbuf, recvbuf, 0)
    exchanged(sendbuf, recvbuf, 0)

    wide = iota((128, 128), 1)
    for j in range(2):
        for h in range(2):
            got = recvbuf[:, 2 * j + h, :]
            turned[j, 128 * h : 128 * h + 128, :] = got.T
            if h == 1:
                first = got[:, 65:66].astype(jnp.int32)
                for c in range(4):
                    onehot_z[256 * c + 128 * j : 256 * c + 128 * j + 128, :] = jnp.where(
                        wide == first + c, 1.0, 0.0
                    ).astype(BF16)
    sub = iota((8, 128), 0)
    bits, inside = [], []
    for j in range(2):
        y_first = jnp.broadcast_to(turned[j, 192:193, :].astype(jnp.int32), (8, 128))
        bits.append([(y_first & n) != 0 for n in (1, 2, 4)])
        offs = [sub + 8 * v - y_first for v in range(4)]
        inside.append([(off >= 0) & (off < 4) for off in offs])

    def place(ka, _):
        rows = pl.ds(pl.multiple_of(ka * 32, 32), 32)
        for c in range(4):
            for j in range(2):
                x = turned[j, pl.ds(ka * 16 + c, 8, stride=4), :]
                for n, bit in zip((1, 2, 4), bits[j]):
                    x = jnp.where(bit, pltpu.roll(x, n, 0), x)
                hi = x.astype(BF16).astype(F32)
                lo = x - hi
                start = 256 * c + 128 * j
                for piece, ref in ((hi, spread_hi), (lo, spread_lo)):
                    ref[rows, start : start + 128] = jnp.concatenate(
                        [jnp.where(inside[j][v], piece, 0.0) for v in range(4)], axis=0
                    ).astype(BF16)
        return 0

    lax.fori_loop(0, 12, place, 0)
    forcing[...] = (dot(spread_hi[...], onehot_z[...]) + dot(spread_lo[...], onehot_z[...])).reshape(3, CX, CY, NZ)

    east, west = (lax.rem(gx + 1, NGX), gy), (lax.rem(gx + NGX - 1, NGX), gy)
    up, down_ = lax.rem(gy + 1, NGY), lax.rem(gy + NGY - 1, NGY)
    north, south = (gx, up), (gx, down_)
    corners = ((7, (east[0], up)), (8, (west[0], down_)), (9, (east[0], down_)), (10, (west[0], up)))

    zlane = iota((8, NZ), 1)
    ysub = iota((8, NZ), 0)
    at_low, at_high = gy == 0, gy == NGY - 1

    def pulled(pad, d, x, yc):
        ex, ey, ez = VEL[d]
        value = pad[AT[d], x + 1 - ex, TOP + 8 * yc - ey : TOP + 8 * yc - ey + 8, :]
        wall = []
        if ez:
            value = pltpu.roll(value, 1 if ez == 1 else NZ - 1, 1)
            wall.append(zlane == (0 if ez == 1 else NZ - 1))
        if ey == 1 and yc == 0:
            wall.append((ysub == 0) & at_low)
        if ey == -1 and yc == 3:
            wall.append((ysub == 7) & at_high)
        if wall:
            mask = wall[0] if len(wall) == 1 else wall[0] | wall[1]
            value = jnp.where(mask, pad[AT[OPP[d]], x + 1, TOP + 8 * yc : TOP + 8 * yc + 8, :], value)
        return value

    def collided(pad, f, x, yc):
        at = slice(8 * yc, 8 * yc + 8)
        out = collide(f, [forcing[k, x, at, :] for k in range(3)])
        for d in range(19):
            pad[AT[d], x + 1, TOP + 8 * yc : TOP + 8 * yc + 8, :] = out[d]

    def halo(pad, n):
        def copy(source, target, i, device):
            return pltpu.make_async_remote_copy(
                source, target, halo_send.at[n, i], halo_recv.at[n, i], device_id=device, device_id_type=MESH
            )

        rows = pl.ds(TOP, CY)
        copies = [
            copy(pad.at[0:5, CX, rows, :], pad.at[0:5, 0, rows, :], 0, east),
            copy(pad.at[5:10, 1, rows, :], pad.at[5:10, CX + 1, rows, :], 1, west),
        ]
        for c in copies:
            c.start()
        for side, dirs, edge, device in ((0, YP, TOP + CY - 1, north), (1, YM, TOP, south)):
            for i, d in enumerate(dirs):
                for x in range(CX):
                    ysend[n, side, i, x : x + 1, :] = pad[AT[d], x + 1, edge : edge + 1, :]
            c = copy(ysend.at[n, side], yrecv.at[n, side], 2 + side, device)
            c.start()
            copies.append(c)
        for i, (d, device) in enumerate(corners):
            x = CX if VEL[d][0] == 1 else 1
            y = TOP + CY - 1 if VEL[d][1] == 1 else TOP
            csend[n, i] = pad[AT[d], x, y : y + 1, :]
            c = copy(csend.at[n, i], crecv.at[n, i], 4 + i, device)
            c.start()
            copies.append(c)
        for c in copies:
            c.wait()
        for side, dirs, edge in ((0, YP, TOP - 1), (1, YM, TOP + CY)):
            for i, d in enumerate(dirs):
                for x in range(CX):
                    pad[AT[d], x + 1, edge : edge + 1, :] = yrecv[n, side, i, x : x + 1, :]
        for i, (d, device) in enumerate(corners):
            x = 0 if VEL[d][0] == 1 else CX + 1
            y = TOP - 1 if VEL[d][1] == 1 else TOP + CY
            pad[AT[d], x, y : y + 1, :] = crecv[n, i]

    def step1(x, _):
        for yc in range(4):
            collided(pad1, [pop[d, x, 8 * yc : 8 * yc + 8, :] for d in range(19)], x, yc)
        return 0

    lax.fori_loop(0, CX, step1, 0)
    halo(pad1, 0)

    def step2(x, _):
        for yc in range(4):
            collided(pad2, [pulled(pad1, d, x, yc) for d in range(19)], x, yc)
        return 0

    lax.fori_loop(0, CX, step2, 0)
    halo(pad2, 1)

    def step3(x, _):
        parts = [[], [], []]
        for yc in range(4):
            f = [pulled(pad2, d, x, yc) for d in range(19)]
            at = slice(8 * yc, 8 * yc + 8)
            for d in range(19):
                new_pop[d, x, at, :] = f[d]
            rho, mom = moments(f)
            inv = 1.0 / rho
            for k in range(3):
                parts[k].append((mom[k] + 0.5 * forcing[k, x, at, :]) * inv)
        for k in range(3):
            fluid[pl.ds(pl.multiple_of(k * 128 + x * 32, 32), 32), :] = jnp.concatenate(parts[k], axis=0).astype(BF16)
        return 0

    lax.fori_loop(0, CX, step3, 0)

    sampled[...] = dot_nt(fluid[...], onehot_z[...])
    for j in range(2):
        samples[j, 192:256, :] = jnp.zeros((64, 128), F32)

    def sample(ka, _):
        for c in range(4):
            for j in range(2):
                cols = slice(256 * c + 128 * j, 256 * c + 128 * j + 128)
                x = sampled[pl.ds(pl.multiple_of(ka * 32, 32), 8), cols]
                for v in range(1, 4):
                    x = jnp.where(inside[j][v], sampled[pl.ds(pl.multiple_of(ka * 32 + 8 * v, 8), 8), cols], x)
                for n, bit in zip((1, 2, 4), bits[j]):
                    x = jnp.where(bit, pltpu.roll(x, 8 - n, 0), x)
                samples[j, pl.ds(ka * 16 + c, 4, stride=4), :] = x[0:4]
        return 0

    lax.fori_loop(0, 12, sample, 0)
    for j in range(2):
        for h in range(2):
            backbuf[:, 2 * j + h, :] = samples[j, 128 * h : 128 * h + 128, :].T
    exchange(backbuf, finbuf, 1)
    exchanged(backbuf, finbuf, 1)

    back = jnp.concatenate(
        [jnp.concatenate([finbuf[:, 2 * j + h, :] for h in range(2)], axis=1) for j in range(2)], axis=0
    ).astype(BF16)
    take = jnp.where(iota((HELD, 256), 1) == slot_col, 1.0, 0.0).astype(BF16)
    cells = dot(take, back)
    means = [[], [], []]
    for g in range(6):
        at = slice(8 * g, 8 * g + 8)
        pair, third = cells[at, 0:128], cells[at, 128:256]
        swapped = pltpu.roll(pair, 64, 1)
        each = (jnp.where(left, pair, swapped), jnp.where(left, swapped, pair), jnp.where(left, third, pltpu.roll(third, 64, 1)))
        lhs = jnp.concatenate(
            [jnp.where(ownpart, jnp.concatenate([e] * 4, axis=1), 0.0) for e in each], axis=0
        ).astype(BF16)
        result = 20.0 * dot(lhs, weights[512 * g : 512 * g + 512, :])
        for k in range(3):
            part = result[8 * k : 8 * k + 8]
            speed_out[at, k, :] = part
            means[k].append(jnp.sum(part, axis=1, keepdims=True) * (1.0 / 128.0))
    mine = jnp.sum(jnp.where(down == across, swimmer[...], 0), axis=1, keepdims=True)
    member = jnp.where(lax.rem(mine, 4) == iota((HELD, 4), 1), 1.0, 0.0)
    swim_out[...] = jnp.concatenate(
        [jnp.sum(jnp.concatenate(means[k], axis=0) * member, axis=0, keepdims=True) for k in range(3)], axis=0
    )


def body(populations, marker_weights, marker_force, owner_device, stencil_base, block_swimmer):
    vmem = pl.BlockSpec(memory_space=pltpu.VMEM)
    return pl.pallas_call(
        kernel,
        out_shape=(
            jax.ShapeDtypeStruct((19, CX, CY, NZ), F32),
            jax.ShapeDtypeStruct((HELD, 3, 128), F32),
            jax.ShapeDtypeStruct((3, 4), F32),
        ),
        in_specs=[vmem] * 6,
        out_specs=(vmem,) * 3,
        scratch_shapes=[
            pltpu.VMEM((NDEV, 4, 128), F32),
            pltpu.VMEM((NDEV, 4, 128), F32),
            pltpu.VMEM((NDEV, 4, 128), F32),
            pltpu.VMEM((NDEV, 4, 128), F32),
            pltpu.VMEM((2, 256, 128), F32),
            pltpu.VMEM((384, 1024), BF16),
            pltpu.VMEM((384, 1024), BF16),
            pltpu.VMEM((1024, 128), BF16),
            pltpu.VMEM((3, CX, CY, NZ), F32),
            pltpu.VMEM((19, CX + 2, CY + 16, NZ), F32),
            pltpu.VMEM((19, CX + 2, CY + 16, NZ), F32),
            pltpu.VMEM((384, 128), BF16),
            pltpu.VMEM((384, 1024), F32),
            pltpu.VMEM((2, 256, 128), F32),
            pltpu.VMEM((2, 2, 5, 4, 128), F32),
            pltpu.VMEM((2, 2, 5, 4, 128), F32),
            pltpu.VMEM((2, 4, 1, 128), F32),
            pltpu.VMEM((2, 4, 1, 128), F32),
            pltpu.SemaphoreType.DMA((2,)),
            pltpu.SemaphoreType.DMA((2,)),
            pltpu.SemaphoreType.DMA((2, 8)),
            pltpu.SemaphoreType.DMA((2, 8)),
        ],
        compiler_params=pltpu.CompilerParams(
            collective_id=0, has_side_effects=True, vmem_limit_bytes=40 * 1024 * 1024
        ),
    )(
        populations,
        marker_weights.reshape(HELD * 64, 128),
        marker_force,
        owner_device,
        stencil_base,
        block_swimmer.reshape(1, HELD),
    )


def solution(mesh):
    in_specs = (
        P(None, "gx", "gy", None),
        P(("gx", "gy"), None, None),
        P(("gx", "gy"), None, None),
        P(("gx", "gy"), None),
        P(("gx", "gy"), None),
        P(("gx", "gy")),
    )
    out_specs = (P(None, "gx", "gy", None), P(("gx", "gy"), None, None), P(None, ("gx", "gy")))
    return jax.shard_map(body, mesh=mesh, in_specs=in_specs, out_specs=out_specs, check_vma=False)
```

time: 2300 us -> 50.4 us (0.02)
  loops' own time: 945 us -> 0 us
  local copies, waits for them, and re-layouts: 805 us -> 7.62 us
  starting transfers between devices: 446 us -> 0 us
  other arithmetic: 55.1 us -> 0 us
  Pallas kernels: 0 us -> 41.7 us
  waiting for transfers between devices: 27 us -> 0 us
    another operation x1 -> x0, loops' own time: 945 us -> none  [body(): lax.scan(place_patch, jnp.zeros((3, slab_cells, strip_cells, height), jnp...]
    dynamic_update_slice x256 -> x0, local copies, waits for them, and re-layouts: 572 us -> none  [place_patch(): lax.dynamic_update_slice(force_grid, existing + patch.reshape(3, STEN, ST...]
    ppermute x8 -> x0, starting transfers between devices: 420 us -> none  [the longest x4 419 us: with_halo(): lax.ppermute(lax.slice_in_dim(block, 0, width, axis=dim), axis, backward)]
    slice x258 -> x0, local copies, waits for them, and re-layouts: 133 us -> none  [the longest x256 133 us: place_patch(): start = (anchor_zero, corner_row[0], corner_row[1], corner_row[2])]
    pallas_call x0 -> x1, Pallas kernels: none -> 41.7 us  [body(): pl.pallas_call(kernel, out_shape=(jax.ShapeDtypeStruct((19, CX, CY, NZ),...]
    gather x21 -> x0, local copies, waits for them, and re-layouts: 31.5 us -> none  [the longest x2 15.6 us: sample_cube(): lax.dynamic_slice(velocity_field, start, (3, STEN, STEN, STEN))]
    reshape x257 -> x0, local copies, waits for them, and re-layouts: 26.1 us -> none  [the longest x256 24.4 us: place_patch(): patch.reshape(3, STEN, STEN, STEN)]
    all_to_all x2 -> x0, starting transfers between devices: 26 us -> none  [the longest x1 14.5 us: body(): lax.all_to_all(gathered_speed.astype(jnp.bfloat16), ('gx', 'gy'), split_a...]
  transfers between devices with their start and end apart: 10 -> 0, of which waited for: 9 -> 0; matrix products, arithmetic and copies ran while one was open for 0% -> 0% of each run, Pallas kernels for 0% -> 0%
where the time goes in v1:
time: 50.4 us; the launch traced here: 50 us
  Pallas kernels  41.7 us (83%)
  local copies, waits for them, and re-layouts  7.62 us (15%)
  between operations  0.65 us (1%)
    pallas_call x1, Pallas kernels, body(): pl.pallas_call(kernel, out_shape=(jax.ShapeDtypeStruct((19, CX, CY, NZ),...  41.7 us
    unnamed x11, local copies, waits for them, and re-layouts  6.98 us

profile of v1, /device:TPU:1, one launch (start us, length us, event | category | flops | bytes accessed | tf_op | source)
XLA Modules:
  0.0 50.0 jit_solution(17818580232936566672)
XLA Ops:
  0.6 0.7 %copy.10.owner = s32[48,1]{1,0:T(8,128)S(1)} copy(s32[48,1]{0,1:T(1,128)} %param.9) | data formatting | bytes 384 | tf_op args[3]
  1.4 0.8 %copy.11.base = s32[48,3]{1,0:T(8,128)S(1)} copy(s32[48,3]{0,1:T(4,128)} %param.10) | data formatting | bytes 1152 | tf_op args[4]
  2.1 0.8 %copy.9.force = bf16[48,3,128]{2,1,0:T(4,128)(2,1)S(1)} copy(bf16[48,3,128]{2,0,1:T(8,128)(2,1)} %param.8) | data formatting | bytes 73728 | tf_op args[2]
  2.9 0.0 copy-start
  2.9 1.3 %copy-done = f32[19,4,32,128]{3,2,1,0:T(8,128)S(1)} copy-done((f32[19,4,32,128]{3,2,1,0:T(8,128)S(1)}, f32[19,4,32,128]{3,2,1,0:T(8,128)}, u32[]{:S(2)}) %copy-start) | copy-done | bytes 1245208
  4.2 0.0 copy-start.1
  4.2 1.1 %copy-done.1 = bf16[48,64,128]{2,1,0:T(8,128)(2,1)S(1)} copy-done((bf16[48,64,128]{2,1,0:T(8,128)(2,1)S(1)}, bf16[48,64,128]{2,1,0:T(8,128)(2,1)}, u32[]{:S(2)}) %copy-start.1) | copy-done | bytes 786456
  5.4 0.0 copy-start.2
  5.4 0.7 %copy-done.2 = s32[48]{0:T(128)S(1)} copy-done((s32[48]{0:T(128)S(1)}, s32[48]{0:T(128)}, u32[]{:S(2)}) %copy-start.2) | copy-done | bytes 216
  6.0 41.7 %shard_map.85 = (f32[19,4,32,128]{3,2,1,0:T(8,128)S(1)}, f32[48,3,128]{2,1,0:T(4,128)S(1)}, f32[3,4]{1,0:T(4,128)S(1)}) custom-call(f32[19,4,32,128]{3,2,1,0:T(8,128)S(1)} %copy-done, bf16[3072,128]{1,0:T(8,128)(2,1)S(1)} %bitcast.2, bf16[48,3,128]{2,1,0:T(4,128)(2,1)S(1)} %copy.9.force, s32[48,1]{1,0:T(8,128)S(1)} %copy.10.owner, s32[48,3]{1,0:T(8,128)S(1)} %copy.11.base, ...), custom_call_target="tpu_custom_call" | custom-call | tf_op jit(solution)/shard_map/pallas_call | solution.py:361
  47.7 0.6 %copy.12 = f32[48,3,128]{2,0,1:T(8,128)} copy(f32[48,3,128]{2,1,0:T(4,128)S(1)} %get-tuple-element.4) | data formatting | bytes 147456 | tf_op jit(solution)/shard_map/pallas_call | solution.py:361
  48.3 1.0 %copy.15 = f32[19,4,32,128]{3,2,1,0:T(8,128)} copy(f32[19,4,32,128]{3,2,1,0:T(8,128)S(1)} %get-tuple-element.9) | data formatting | bytes 2490368
  49.4 0.6 %copy.16 = f32[3,4]{1,0:T(4,128)} copy(f32[3,4]{1,0:T(4,128)S(1)} %get-tuple-element.11) | data formatting | bytes 96
Async XLA Ops:
  2.9 1.3 %copy-start = (f32[19,4,32,128]{3,2,1,0:T(8,128)S(1)}, f32[19,4,32,128]{3,2,1,0:T(8,128)}, u32[]{:S(2)}) copy-start(f32[19,4,32,128]{3,2,1,0:T(8,128)} %pop.1) | copy-start | bytes 3735556
  4.2 1.1 %copy-start.1 = (bf16[48,64,128]{2,1,0:T(8,128)(2,1)S(1)}, bf16[48,64,128]{2,1,0:T(8,128)(2,1)}, u32[]{:S(2)}) copy-start(bf16[48,64,128]{2,1,0:T(8,128)(2,1)} %param.7) | copy-start | bytes 2359300
  5.4 0.7 %copy-start.2 = (s32[48]{0:T(128)S(1)}, s32[48]{0:T(128)}, u32[]{:S(2)}) copy-start(s32[48]{0:T(128)} %param.11) | copy-start | bytes 580

commit v2 on v1

--- a/solution.py
+++ b/solution.py
@@ -88,28 +88,57 @@
 
 
 def kernel(
+    pop_hbm, weights_hbm, force_hbm, owner_hbm, base_hbm, swimmer_hbm,
+    new_pop, speed_out, swim_out,
     pop, weights, force, owner, base, swimmer,
-    new_pop, speed_out, swim_out,
     sendbuf, recvbuf, backbuf, finbuf, turned, spread_hi, spread_lo, onehot_z, forcing, pad1, pad2, fluid, sampled, samples,
     ysend, yrecv, csend, crecv,
-    send_sem, recv_sem, halo_send, halo_recv,
+    load_sem, send_sem, recv_sem, halo_send, halo_recv,
 ):
+    loads = [
+        pltpu.make_async_copy(source, target, load_sem.at[i])
+        for i, (source, target) in enumerate(
+            ((owner_hbm, owner), (base_hbm, base), (force_hbm, force), (weights_hbm, weights), (swimmer_hbm, swimmer), (pop_hbm, pop))
+        )
+    ]
+    for load in loads:
+        load.start()
+
     gx, gy = lax.axis_index("gx"), lax.axis_index("gy")
     me = gx * NGY + gy
+    core, my_x = lax.rem(gx, 2), lax.rem(lax.div(gx, 2), 4)
+    my_y, my_z = lax.div(gy, 2), lax.div(gx, 8) * 2 + lax.rem(gy, 2)
+
+    def chip(dx, dy, dz):
+        z = lax.rem(my_z + dz, 4)
+        return lax.div(z, 2) * 8 + lax.rem(my_x + dx, 4) * 2, lax.rem(my_y + dy, 4) * 2 + lax.rem(z, 2)
+
+    def to_all(act):
+        def offset(digit):
+            return jnp.where(digit < 2, 2 * digit + 1, 6 - 2 * digit)
+
+        def step(i, _):
+            tx, ty = chip(offset(lax.rem(i, 4)), offset(lax.rem(lax.div(i, 4), 4)), offset(lax.div(i, 16)))
+            act(tx, ty)
+            act(tx + 1, ty)
+            return 0
+
+        lax.fori_loop(0, 63, step, 0)
+        act(gx + 1 - 2 * core, gy)
 
     barrier = pltpu.get_barrier_semaphore()
-
-    def greet(i, _):
-        t = lax.rem(me + i, NDEV)
-        pl.semaphore_signal(barrier, inc=1, device_id=(t // NGY, lax.rem(t, NGY)), device_id_type=MESH)
-        return 0
-
-    lax.fori_loop(1, NDEV, greet, 0)
-
-    col = owner[...]
+    to_all(lambda tx, ty: pl.semaphore_signal(barrier, inc=1, device_id=(tx, ty), device_id_type=MESH))
+
+    for load in loads[:4]:
+        load.wait()
     square = (HELD, HELD)
     down, across = iota(square, 0), iota(square, 1)
-    row = jnp.sum(jnp.where(down == across, col, 0), axis=0, keepdims=True)
+
+    def standing(line):
+        return jnp.sum(jnp.where(down == across, line, 0), axis=1, keepdims=True)
+
+    row = owner[...]
+    col = standing(row)
     same = col == row
     rank_col = jnp.sum(jnp.where(same & (across < down), 1, 0), axis=1, keepdims=True)
     rank_row = jnp.sum(jnp.where(same & (down < across), 1, 0), axis=0, keepdims=True)
@@ -119,9 +148,9 @@
     lane = iota((8, 128), 1)
     left = lane < 64
     ownpart = iota((8, 512), 1) // 64 == iota((8, 512), 0)
-    pulls = force[...].astype(F32)
-    pulls = [pulls[:, k, :] for k in range(3)]
-    corner = base[...].astype(F32)
+    pulls = [force[k].astype(F32) for k in range(3)]
+    strip = standing(base[1:2, :]).astype(F32)
+    column = standing(base[2:3, :]).astype(F32)
     rows01, rows2x = [], []
     for g in range(6):
         at = slice(8 * g, 8 * g + 8)
@@ -132,7 +161,7 @@
             x = jnp.where(ownpart, full[8 * k : 8 * k + 8], 0.0)
             y = (x[:, 0:128] + x[:, 128:256]) + (x[:, 256:384] + x[:, 384:512])
             part.append(y + pltpu.roll(y, 64, 1))
-        extra = jnp.where(lane == 64, corner[at, 1:2], jnp.where(lane == 65, corner[at, 2:3], 0.0))
+        extra = jnp.where(lane == 64, strip[at], jnp.where(lane == 65, column[at], 0.0))
         rows01.append(jnp.where(left, part[0], part[1]))
         rows2x.append(jnp.where(left, part[2], extra))
     patch = jnp.concatenate([jnp.concatenate(rows01, axis=0), jnp.concatenate(rows2x, axis=0)], axis=1)
@@ -147,25 +176,22 @@
     pl.semaphore_wait(barrier, NDEV - 1)
 
     def exchange(source, target, n):
-        def send(i, _):
-            t = lax.rem(me + i, NDEV)
-            pltpu.make_async_remote_copy(
-                source.at[t], target.at[me], send_sem.at[n], recv_sem.at[n],
-                device_id=(t // NGY, lax.rem(t, NGY)), device_id_type=MESH,
+        to_all(
+            lambda tx, ty: pltpu.make_async_remote_copy(
+                source.at[tx * NGY + ty], target.at[me], send_sem.at[n], recv_sem.at[n],
+                device_id=(tx, ty), device_id_type=MESH,
             ).start()
-            return 0
-
-        lax.fori_loop(1, NDEV, send, 0)
+        )
         target[me] = source[me]
 
     def exchanged(source, target, n):
-        pltpu.make_async_remote_copy(
+        return pltpu.make_async_remote_copy(
             source.at[pl.ds(0, NDEV - 1)], target.at[pl.ds(0, NDEV - 1)], send_sem.at[n], recv_sem.at[n],
             device_id=(lax.rem(gx + 1, NGX), gy), device_id_type=MESH,
-        ).wait()
+        )
 
     exchange(sendbuf, recvbuf, 0)
-    exchanged(sendbuf, recvbuf, 0)
+    exchanged(sendbuf, recvbuf, 0).wait_recv()
 
     wide = iota((128, 128), 1)
     for j in range(2):
@@ -236,35 +262,33 @@
         for d in range(19):
             pad[AT[d], x + 1, TOP + 8 * yc : TOP + 8 * yc + 8, :] = out[d]
 
-    def halo(pad, n):
+    def halo_start(pad, n):
         def copy(source, target, i, device):
-            return pltpu.make_async_remote_copy(
+            c = pltpu.make_async_remote_copy(
                 source, target, halo_send.at[n, i], halo_recv.at[n, i], device_id=device, device_id_type=MESH
             )
+            c.start()
+            return c
 
         rows = pl.ds(TOP, CY)
-        copies = [
-            copy(pad.at[0:5, CX, rows, :], pad.at[0:5, 0, rows, :], 0, east),
-            copy(pad.at[5:10, 1, rows, :], pad.at[5:10, CX + 1, rows, :], 1, west),
-        ]
-        for c in copies:
-            c.start()
+        copies = []
+        for i, (d, device) in enumerate(corners):
+            x = CX if VEL[d][0] == 1 else 1
+            y = TOP + CY - 1 if VEL[d][1] == 1 else TOP
+            csend[n, i] = pad[AT[d], x, y : y + 1, :]
+            copies.append(copy(csend.at[n, i], crecv.at[n, i], 4 + i, device))
+        copies.append(copy(pad.at[0:5, CX, rows, :], pad.at[0:5, 0, rows, :], 0, east))
+        copies.append(copy(pad.at[5:10, 1, rows, :], pad.at[5:10, CX + 1, rows, :], 1, west))
         for side, dirs, edge, device in ((0, YP, TOP + CY - 1, north), (1, YM, TOP, south)):
             for i, d in enumerate(dirs):
                 for x in range(CX):
                     ysend[n, side, i, x : x + 1, :] = pad[AT[d], x + 1, edge : edge + 1, :]
-            c = copy(ysend.at[n, side], yrecv.at[n, side], 2 + side, device)
-            c.start()
-            copies.append(c)
-        for i, (d, device) in enumerate(corners):
-            x = CX if VEL[d][0] == 1 else 1
-            y = TOP + CY - 1 if VEL[d][1] == 1 else TOP
-            csend[n, i] = pad[AT[d], x, y : y + 1, :]
-            c = copy(csend.at[n, i], crecv.at[n, i], 4 + i, device)
-            c.start()
-            copies.append(c)
+            copies.append(copy(ysend.at[n, side], yrecv.at[n, side], 2 + side, device))
+        return copies
+
+    def halo_finish(pad, n, copies):
         for c in copies:
-            c.wait()
+            c.wait_recv()
         for side, dirs, edge in ((0, YP, TOP - 1), (1, YM, TOP + CY)):
             for i, d in enumerate(dirs):
                 for x in range(CX):
@@ -274,40 +298,57 @@
             y = TOP - 1 if VEL[d][1] == 1 else TOP + CY
             pad[AT[d], x, y : y + 1, :] = crecv[n, i]
 
-    def step1(x, _):
-        for yc in range(4):
-            collided(pad1, [pop[d, x, 8 * yc : 8 * yc + 8, :] for d in range(19)], x, yc)
-        return 0
-
-    lax.fori_loop(0, CX, step1, 0)
-    halo(pad1, 0)
-
-    def step2(x, _):
-        for yc in range(4):
-            collided(pad2, [pulled(pad1, d, x, yc) for d in range(19)], x, yc)
-        return 0
-
-    lax.fori_loop(0, CX, step2, 0)
-    halo(pad2, 1)
-
-    def step3(x, _):
-        parts = [[], [], []]
-        for yc in range(4):
-            f = [pulled(pad2, d, x, yc) for d in range(19)]
-            at = slice(8 * yc, 8 * yc + 8)
-            for d in range(19):
-                new_pop[d, x, at, :] = f[d]
-            rho, mom = moments(f)
-            inv = 1.0 / rho
-            for k in range(3):
-                parts[k].append((mom[k] + 0.5 * forcing[k, x, at, :]) * inv)
+    def rim(work):
+        def sides(i, _):
+            for yc in range(4):
+                work(i * (CX - 1), yc)
+            return 0
+
+        def middle(x, _):
+            work(x, 0)
+            work(x, 3)
+            return 0
+
+        lax.fori_loop(0, 2, sides, 0)
+        lax.fori_loop(1, CX - 1, middle, 0)
+
+    def core_cells(work):
+        def middle(x, _):
+            work(x, 1)
+            work(x, 2)
+            return 0
+
+        lax.fori_loop(1, CX - 1, middle, 0)
+
+    def step1(x, yc):
+        collided(pad1, [pop[d, x, 8 * yc : 8 * yc + 8, :] for d in range(19)], x, yc)
+
+    def step2(x, yc):
+        collided(pad2, [pulled(pad1, d, x, yc) for d in range(19)], x, yc)
+
+    def step3(x, yc):
+        f = [pulled(pad2, d, x, yc) for d in range(19)]
+        at = slice(8 * yc, 8 * yc + 8)
+        for d in range(19):
+            new_pop[d, x, at, :] = f[d]
+        rho, mom = moments(f)
+        inv = 1.0 / rho
         for k in range(3):
-            fluid[pl.ds(pl.multiple_of(k * 128 + x * 32, 32), 32), :] = jnp.concatenate(parts[k], axis=0).astype(BF16)
-        return 0
-
-    lax.fori_loop(0, CX, step3, 0)
-
-    sampled[...] = dot_nt(fluid[...], onehot_z[...])
+            fluid[k, x, at, :] = (mom[k] + 0.5 * forcing[k, x, at, :]) * inv
+
+    loads[5].wait()
+    rim(step1)
+    halo1 = halo_start(pad1, 0)
+    core_cells(step1)
+    core_cells(step2)
+    halo_finish(pad1, 0, halo1)
+    rim(step2)
+    halo2 = halo_start(pad2, 1)
+    core_cells(step3)
+    halo_finish(pad2, 1, halo2)
+    rim(step3)
+
+    sampled[...] = dot_nt(fluid[...].reshape(384, NZ).astype(BF16), onehot_z[...])
     for j in range(2):
         samples[j, 192:256, :] = jnp.zeros((64, 128), F32)
 
@@ -328,7 +369,7 @@
         for h in range(2):
             backbuf[:, 2 * j + h, :] = samples[j, 128 * h : 128 * h + 128, :].T
     exchange(backbuf, finbuf, 1)
-    exchanged(backbuf, finbuf, 1)
+    exchanged(backbuf, finbuf, 1).wait_recv()
 
     back = jnp.concatenate(
         [jnp.concatenate([finbuf[:, 2 * j + h, :] for h in range(2)], axis=1) for j in range(2)], axis=0
@@ -347,27 +388,48 @@
         result = 20.0 * dot(lhs, weights[512 * g : 512 * g + 512, :])
         for k in range(3):
             part = result[8 * k : 8 * k + 8]
-            speed_out[at, k, :] = part
+            speed_out[k, at, :] = part
             means[k].append(jnp.sum(part, axis=1, keepdims=True) * (1.0 / 128.0))
-    mine = jnp.sum(jnp.where(down == across, swimmer[...], 0), axis=1, keepdims=True)
+    loads[4].wait()
+    mine = standing(swimmer[...])
     member = jnp.where(lax.rem(mine, 4) == iota((HELD, 4), 1), 1.0, 0.0)
     swim_out[...] = jnp.concatenate(
         [jnp.sum(jnp.concatenate(means[k], axis=0) * member, axis=0, keepdims=True) for k in range(3)], axis=0
     )
 
+    exchanged(sendbuf, recvbuf, 0).wait_send()
+    exchanged(backbuf, finbuf, 1).wait_send()
+    for c in halo1 + halo2:
+        c.wait_send()
+
 
 def body(populations, marker_weights, marker_force, owner_device, stencil_base, block_swimmer):
     vmem = pl.BlockSpec(memory_space=pltpu.VMEM)
-    return pl.pallas_call(
+    hbm = pl.BlockSpec(memory_space=pl.ANY)
+    operands = (
+        populations,
+        marker_weights.reshape(HELD * 64, 128),
+        marker_force.transpose(1, 0, 2),
+        owner_device.reshape(1, HELD),
+        stencil_base.T,
+        block_swimmer.reshape(1, HELD),
+    )
+    fields, speed, swim = pl.pallas_call(
         kernel,
         out_shape=(
             jax.ShapeDtypeStruct((19, CX, CY, NZ), F32),
-            jax.ShapeDtypeStruct((HELD, 3, 128), F32),
+            jax.ShapeDtypeStruct((3, HELD, 128), F32),
             jax.ShapeDtypeStruct((3, 4), F32),
         ),
-        in_specs=[vmem] * 6,
+        in_specs=[hbm] * 6,
         out_specs=(vmem,) * 3,
         scratch_shapes=[
+            pltpu.VMEM((19, CX, CY, NZ), F32),
+            pltpu.VMEM((HELD * 64, 128), BF16),
+            pltpu.VMEM((3, HELD, 128), BF16),
+            pltpu.VMEM((1, HELD), jnp.int32),
+            pltpu.VMEM((3, HELD), jnp.int32),
+            pltpu.VMEM((1, HELD), jnp.int32),
             pltpu.VMEM((NDEV, 4, 128), F32),
             pltpu.VMEM((NDEV, 4, 128), F32),
             pltpu.VMEM((NDEV, 4, 128), F32),
@@ -379,13 +441,14 @@
             pltpu.VMEM((3, CX, CY, NZ), F32),
             pltpu.VMEM((19, CX + 2, CY + 16, NZ), F32),
             pltpu.VMEM((19, CX + 2, CY + 16, NZ), F32),
-            pltpu.VMEM((384, 128), BF16),
+            pltpu.VMEM((3, CX, CY, NZ), F32),
             pltpu.VMEM((384, 1024), F32),
             pltpu.VMEM((2, 256, 128), F32),
             pltpu.VMEM((2, 2, 5, 4, 128), F32),
             pltpu.VMEM((2, 2, 5, 4, 128), F32),
             pltpu.VMEM((2, 4, 1, 128), F32),
             pltpu.VMEM((2, 4, 1, 128), F32),
+            pltpu.SemaphoreType.DMA((6,)),
             pltpu.SemaphoreType.DMA((2,)),
             pltpu.SemaphoreType.DMA((2,)),
             pltpu.SemaphoreType.DMA((2, 8)),
@@ -395,13 +458,9 @@
             collective_id=0, has_side_effects=True, vmem_limit_bytes=40 * 1024 * 1024
         ),
     )(
-        populations,
-        marker_weights.reshape(HELD * 64, 128),
-        marker_force,
-        owner_device,
-        stencil_base,
-        block_swimmer.reshape(1, HELD),
+        *(pltpu.with_memory_space_constraint(x, pltpu.HBM) for x in operands)
     )
+    return fields, speed.transpose(1, 0, 2), swim
 
 
 def solution(mesh):

time: 50.4 us -> 44.8 us (0.89)
  local copies, waits for them, and re-layouts: 7.62 us -> 2.25 us
    unnamed x11 -> x3, local copies, waits for them, and re-layouts: 6.98 us -> 2.25 us
    pallas_call x1 -> x0, local copies, waits for them, and re-layouts: 0.64 us -> none  [body(): pl.pallas_call(kernel, out_shape=(jax.ShapeDtypeStruct((19, CX, CY, NZ),...]
where the time goes in v2:
time: 44.8 us; the launch traced here: 44.7 us
  Pallas kernels  41.8 us (93%)
  local copies, waits for them, and re-layouts  2.25 us (5%)
  between operations  0.64 us (1%)
    pallas_call x1, Pallas kernels, body(): pl.pallas_call(kernel, out_shape=(jax.ShapeDtypeStruct((19, CX, CY, NZ),...  41.8 us
    unnamed x3, local copies, waits for them, and re-layouts  2.25 us

profile of v2, /device:TPU:1, one launch (start us, length us, event | category | flops | bytes accessed | tf_op | source)
XLA Modules:
  0.0 44.7 jit_solution(17021285620428398099)
XLA Ops:
  0.6 41.8 %shard_map.85 = (f32[19,4,32,128]{3,2,1,0:T(8,128)S(1)}, f32[3,48,128]{2,1,0:T(8,128)S(1)}, f32[3,4]{1,0:T(4,128)S(1)}) custom-call(f32[19,4,32,128]{3,2,1,0:T(8,128)} %pop_hbm.1, bf16[3072,128]{1,0:T(8,128)(2,1)} %bitcast.7, bf16[3,48,128]{2,1,0:T(8,128)(2,1)} %bitcast.8, s32[1,48]{1,0:T(1,128)} %bitcast.10, s32[3,48]{1,0:T(4,128)} %bitcast.9, s32[1,48]{1,0:T(1,128)} %bitcast.11), custom_call_target="tpu_custom_call" | custom-call | tf_op jit(solution)/shard_map/pallas_call | solution.py:417
  42.4 1.0 %copy.12 = f32[19,4,32,128]{3,2,1,0:T(8,128)} copy(f32[19,4,32,128]{3,2,1,0:T(8,128)S(1)} %get-tuple-element.12) | data formatting | bytes 2490368
  43.5 0.6 %copy.13 = f32[48,3,128]{2,0,1:T(8,128)} copy(f32[48,3,128]{2,0,1:T(8,128)S(1)} %bitcast.6) | data formatting | bytes 147456
  44.1 0.6 %copy.14 = f32[3,4]{1,0:T(4,128)} copy(f32[3,4]{1,0:T(4,128)S(1)} %get-tuple-element.14) | data formatting | bytes 96

commit v3 on v2

--- a/solution.py
+++ b/solution.py
@@ -44,6 +44,10 @@
 
 def dot_nt(a, b):
     return lax.dot_general(a, b, (((1,), (1,)), ((), ())), preferred_element_type=F32)
+
+
+def own_part():
+    return lax.div(iota((8, 512), 1), 64) == iota((8, 512), 0)
 
 
 def moments(f):
@@ -89,9 +93,9 @@
 
 def kernel(
     pop_hbm, weights_hbm, force_hbm, owner_hbm, base_hbm, swimmer_hbm,
-    new_pop, speed_out, swim_out,
-    pop, weights, force, owner, base, swimmer,
-    sendbuf, recvbuf, backbuf, finbuf, turned, spread_hi, spread_lo, onehot_z, forcing, pad1, pad2, fluid, sampled, samples,
+    new_pop, finbuf, weights, take_out, member_out,
+    pop, force, owner, base, swimmer,
+    sendbuf, recvbuf, backbuf, turned, spread_hi, spread_lo, onehot_z, forcing, pad1, pad2, fluid, sampled, samples,
     ysend, yrecv, csend, crecv,
     load_sem, send_sem, recv_sem, halo_send, halo_recv,
 ):
@@ -101,33 +105,38 @@
             ((owner_hbm, owner), (base_hbm, base), (force_hbm, force), (weights_hbm, weights), (swimmer_hbm, swimmer), (pop_hbm, pop))
         )
     ]
-    for load in loads:
-        load.start()
-
     gx, gy = lax.axis_index("gx"), lax.axis_index("gy")
     me = gx * NGY + gy
     core, my_x = lax.rem(gx, 2), lax.rem(lax.div(gx, 2), 4)
     my_y, my_z = lax.div(gy, 2), lax.div(gx, 8) * 2 + lax.rem(gy, 2)
 
-    def chip(dx, dy, dz):
-        z = lax.rem(my_z + dz, 4)
-        return lax.div(z, 2) * 8 + lax.rem(my_x + dx, 4) * 2, lax.rem(my_y + dy, 4) * 2 + lax.rem(z, 2)
+    along_x = [lax.rem(my_x + d, 4) * 2 for d in (1, 3, 2, 0)]
 
     def to_all(act):
         def offset(digit):
             return jnp.where(digit < 2, 2 * digit + 1, 6 - 2 * digit)
 
         def step(i, _):
-            tx, ty = chip(offset(lax.rem(i, 4)), offset(lax.rem(lax.div(i, 4), 4)), offset(lax.div(i, 16)))
-            act(tx, ty)
-            act(tx + 1, ty)
+            z = lax.rem(my_z + offset(lax.div(i, 4)), 4)
+            tx = lax.div(z, 2) * 8
+            ty = lax.rem(my_y + offset(lax.rem(i, 4)), 4) * 2 + lax.rem(z, 2)
+            for x in along_x:
+                act(tx + x, ty)
+                act(tx + x + 1, ty)
             return 0
 
-        lax.fori_loop(0, 63, step, 0)
+        lax.fori_loop(0, 15, step, 0)
+        first = lax.div(gx, 8) * 8
+        for x in along_x[:3]:
+            act(first + x, gy)
+            act(first + x + 1, gy)
         act(gx + 1 - 2 * core, gy)
 
     barrier = pltpu.get_barrier_semaphore()
     to_all(lambda tx, ty: pl.semaphore_signal(barrier, inc=1, device_id=(tx, ty), device_id_type=MESH))
+
+    for load in loads:
+        load.start()
 
     for load in loads[:4]:
         load.wait()
@@ -145,9 +154,13 @@
     slot_row = rank_row * NDEV + row
     slot_col = rank_col * NDEV + col
 
+    take_out[...] = jnp.where(iota((HELD, 256), 1) == slot_col, 1.0, 0.0).astype(BF16)
+    loads[4].wait()
+    member_out[...] = jnp.where(lax.rem(standing(swimmer[...]), 4) == iota((HELD, 4), 1), 1.0, 0.0)
+
     lane = iota((8, 128), 1)
     left = lane < 64
-    ownpart = iota((8, 512), 1) // 64 == iota((8, 512), 0)
+    ownpart = own_part()
     pulls = [force[k].astype(F32) for k in range(3)]
     strip = standing(base[1:2, :]).astype(F32)
     column = standing(base[2:3, :]).astype(F32)
@@ -371,11 +384,28 @@
     exchange(backbuf, finbuf, 1)
     exchanged(backbuf, finbuf, 1).wait_recv()
 
+    exchanged(sendbuf, recvbuf, 0).wait_send()
+    exchanged(backbuf, finbuf, 1).wait_send()
+    for c in halo1 + halo2:
+        c.wait_send()
+
+
+def finish(
+    fields, finbuf, weights, take, member,
+    fields_hbm, speed_hbm, swim_hbm,
+    speed, swim, sem,
+):
+    stores = [
+        pltpu.make_async_copy(source, target, sem.at[i])
+        for i, (source, target) in enumerate(((fields, fields_hbm), (speed, speed_hbm), (swim, swim_hbm)))
+    ]
+    stores[0].start()
+    left = iota((8, 128), 1) < 64
+    ownpart = own_part()
     back = jnp.concatenate(
         [jnp.concatenate([finbuf[:, 2 * j + h, :] for h in range(2)], axis=1) for j in range(2)], axis=0
     ).astype(BF16)
-    take = jnp.where(iota((HELD, 256), 1) == slot_col, 1.0, 0.0).astype(BF16)
-    cells = dot(take, back)
+    cells = dot(take[...], back)
     means = [[], [], []]
     for g in range(6):
         at = slice(8 * g, 8 * g + 8)
@@ -388,19 +418,16 @@
         result = 20.0 * dot(lhs, weights[512 * g : 512 * g + 512, :])
         for k in range(3):
             part = result[8 * k : 8 * k + 8]
-            speed_out[k, at, :] = part
+            speed[k, at, :] = part
             means[k].append(jnp.sum(part, axis=1, keepdims=True) * (1.0 / 128.0))
-    loads[4].wait()
-    mine = standing(swimmer[...])
-    member = jnp.where(lax.rem(mine, 4) == iota((HELD, 4), 1), 1.0, 0.0)
-    swim_out[...] = jnp.concatenate(
-        [jnp.sum(jnp.concatenate(means[k], axis=0) * member, axis=0, keepdims=True) for k in range(3)], axis=0
+    stores[1].start()
+    belongs = member[...]
+    swim[...] = jnp.concatenate(
+        [jnp.sum(jnp.concatenate(means[k], axis=0) * belongs, axis=0, keepdims=True) for k in range(3)], axis=0
     )
-
-    exchanged(sendbuf, recvbuf, 0).wait_send()
-    exchanged(backbuf, finbuf, 1).wait_send()
-    for c in halo1 + halo2:
-        c.wait_send()
+    stores[2].start()
+    for store in stores:
+        store.wait()
 
 
 def body(populations, marker_weights, marker_force, owner_device, stencil_base, block_swimmer):
@@ -414,23 +441,23 @@
         stencil_base.T,
         block_swimmer.reshape(1, HELD),
     )
-    fields, speed, swim = pl.pallas_call(
+    handed = pl.pallas_call(
         kernel,
         out_shape=(
             jax.ShapeDtypeStruct((19, CX, CY, NZ), F32),
-            jax.ShapeDtypeStruct((3, HELD, 128), F32),
-            jax.ShapeDtypeStruct((3, 4), F32),
+            jax.ShapeDtypeStruct((NDEV, 4, 128), F32),
+            jax.ShapeDtypeStruct((HELD * 64, 128), BF16),
+            jax.ShapeDtypeStruct((HELD, 256), BF16),
+            jax.ShapeDtypeStruct((HELD, 4), F32),
         ),
         in_specs=[hbm] * 6,
-        out_specs=(vmem,) * 3,
+        out_specs=(vmem,) * 5,
         scratch_shapes=[
             pltpu.VMEM((19, CX, CY, NZ), F32),
-            pltpu.VMEM((HELD * 64, 128), BF16),
             pltpu.VMEM((3, HELD, 128), BF16),
             pltpu.VMEM((1, HELD), jnp.int32),
             pltpu.VMEM((3, HELD), jnp.int32),
             pltpu.VMEM((1, HELD), jnp.int32),
-            pltpu.VMEM((NDEV, 4, 128), F32),
             pltpu.VMEM((NDEV, 4, 128), F32),
             pltpu.VMEM((NDEV, 4, 128), F32),
             pltpu.VMEM((NDEV, 4, 128), F32),
@@ -460,6 +487,22 @@
     )(
         *(pltpu.with_memory_space_constraint(x, pltpu.HBM) for x in operands)
     )
+    fields, speed, swim = pl.pallas_call(
+        finish,
+        out_shape=(
+            jax.ShapeDtypeStruct((19, CX, CY, NZ), F32),
+            jax.ShapeDtypeStruct((3, HELD, 128), F32),
+            jax.ShapeDtypeStruct((3, 4), F32),
+        ),
+        in_specs=[vmem] * 5,
+        out_specs=(hbm,) * 3,
+        scratch_shapes=[
+            pltpu.VMEM((3, HELD, 128), F32),
+            pltpu.VMEM((3, 4), F32),
+            pltpu.SemaphoreType.DMA((3,)),
+        ],
+        compiler_params=pltpu.CompilerParams(vmem_limit_bytes=16 * 1024 * 1024),
+    )(*handed)
     return fields, speed.transpose(1, 0, 2), swim
 
 

time: 44.8 us -> 41.3 us (0.922)
  local copies, waits for them, and re-layouts: 2.25 us -> 0 us
  Pallas kernels: 41.8 us -> 40.5 us
    pallas_call x1, Pallas kernels: 41.8 us -> 39.2 us  [body(): pl.pallas_call(kernel, out_shape=(jax.ShapeDtypeStruct((19, CX, CY, NZ),...]
    unnamed x3 -> x0, local copies, waits for them, and re-layouts: 2.25 us -> none
    pallas_call x0 -> x1, Pallas kernels: none -> 1.32 us  [body(): pl.pallas_call(finish, out_shape=(jax.ShapeDtypeStruct((19, CX, CY, NZ),...]
where the time goes in v3:
time: 41.3 us; the launch traced here: 41.1 us
  Pallas kernels  40.5 us (98%)
  between operations  0.64 us (2%)
    pallas_call x1, Pallas kernels, body(): pl.pallas_call(kernel, out_shape=(jax.ShapeDtypeStruct((19, CX, CY, NZ),...  39.2 us
    pallas_call x1, Pallas kernels, body(): pl.pallas_call(finish, out_shape=(jax.ShapeDtypeStruct((19, CX, CY, NZ),...  1.32 us

profile of v3, /device:TPU:1, one launch (start us, length us, event | category | flops | bytes accessed | tf_op | source)
XLA Modules:
  0.0 41.1 jit_solution(17585566898461218902)
XLA Ops:
  0.6 39.2 %shard_map.85 = (f32[19,4,32,128]{3,2,1,0:T(8,128)S(1)}, f32[128,4,128]{2,1,0:T(4,128)S(1)}, bf16[3072,128]{1,0:T(8,128)(2,1)S(1)}, bf16[48,256]{1,0:T(8,128)(2,1)S(1)}, f32[48,4]{1,0:T(8,128)S(1)}) custom-call(f32[19,4,32,128]{3,2,1,0:T(8,128)} %pop_hbm.1, bf16[3072,128]{1,0:T(8,128)(2,1)} %bitcast.6, bf16[3,48,128]{2,1,0:T(8,128)(2,1)} %bitcast.7, ...), custom_call_target="tpu_custom_call" | custom-call | tf_op jit(solution)/shard_map/pallas_call | solution.py:444
  39.8 1.3 %shard_map.86 = (f32[19,4,32,128]{3,2,1,0:T(8,128)}, f32[3,48,128]{2,1,0:T(8,128)}, f32[3,4]{1,0:T(4,128)}) custom-call(f32[19,4,32,128]{3,2,1,0:T(8,128)S(1)} %get-tuple-element.11.fields, f32[128,4,128]{2,1,0:T(4,128)S(1)} %get-tuple-element.12.finbuf, bf16[3072,128]{1,0:T(8,128)(2,1)S(1)} %get-tuple-element.13.weights, ...), custom_call_target="tpu_custom_call" | custom-call | tf_op jit(solution)/shard_map/pallas_call | solution.py:490

commit v4 on v3

--- a/solution.py
+++ b/solution.py
@@ -212,10 +212,10 @@
             got = recvbuf[:, 2 * j + h, :]
             turned[j, 128 * h : 128 * h + 128, :] = got.T
             if h == 1:
-                first = got[:, 65:66].astype(jnp.int32)
+                ahead = wide - jnp.broadcast_to(got[:, 65:66], (128, 128)).astype(jnp.int32)
                 for c in range(4):
                     onehot_z[256 * c + 128 * j : 256 * c + 128 * j + 128, :] = jnp.where(
-                        wide == first + c, 1.0, 0.0
+                        ahead == c, 1.0, 0.0
                     ).astype(BF16)
     sub = iota((8, 128), 0)
     bits, inside = [], []
@@ -225,8 +225,8 @@
         offs = [sub + 8 * v - y_first for v in range(4)]
         inside.append([(off >= 0) & (off < 4) for off in offs])
 
-    def place(ka, _):
-        rows = pl.ds(pl.multiple_of(ka * 32, 32), 32)
+    def place(ka):
+        rows = slice(32 * ka, 32 * ka + 32)
         for c in range(4):
             for j in range(2):
                 x = turned[j, pl.ds(ka * 16 + c, 8, stride=4), :]
@@ -239,10 +239,12 @@
                     ref[rows, start : start + 128] = jnp.concatenate(
                         [jnp.where(inside[j][v], piece, 0.0) for v in range(4)], axis=0
                     ).astype(BF16)
-        return 0
-
-    lax.fori_loop(0, 12, place, 0)
-    forcing[...] = (dot(spread_hi[...], onehot_z[...]) + dot(spread_lo[...], onehot_z[...])).reshape(3, CX, CY, NZ)
+
+    for k in range(3):
+        for a in range(CX):
+            place(CX * k + a)
+        rows = slice(128 * k, 128 * k + 128)
+        forcing[k] = (dot(spread_hi[rows, :], onehot_z[...]) + dot(spread_lo[rows, :], onehot_z[...])).reshape(CX, CY, NZ)
 
     east, west = (lax.rem(gx + 1, NGX), gy), (lax.rem(gx + NGX - 1, NGX), gy)
     up, down_ = lax.rem(gy + 1, NGY), lax.rem(gy + NGY - 1, NGY)
@@ -361,23 +363,24 @@
     halo_finish(pad2, 1, halo2)
     rim(step3)
 
-    sampled[...] = dot_nt(fluid[...].reshape(384, NZ).astype(BF16), onehot_z[...])
     for j in range(2):
         samples[j, 192:256, :] = jnp.zeros((64, 128), F32)
 
-    def sample(ka, _):
+    def sample(ka):
         for c in range(4):
             for j in range(2):
                 cols = slice(256 * c + 128 * j, 256 * c + 128 * j + 128)
-                x = sampled[pl.ds(pl.multiple_of(ka * 32, 32), 8), cols]
+                x = sampled[slice(32 * ka, 32 * ka + 8), cols]
                 for v in range(1, 4):
-                    x = jnp.where(inside[j][v], sampled[pl.ds(pl.multiple_of(ka * 32 + 8 * v, 8), 8), cols], x)
+                    x = jnp.where(inside[j][v], sampled[slice(32 * ka + 8 * v, 32 * ka + 8 * v + 8), cols], x)
                 for n, bit in zip((1, 2, 4), bits[j]):
                     x = jnp.where(bit, pltpu.roll(x, 8 - n, 0), x)
                 samples[j, pl.ds(ka * 16 + c, 4, stride=4), :] = x[0:4]
-        return 0
-
-    lax.fori_loop(0, 12, sample, 0)
+
+    for k in range(3):
+        sampled[128 * k : 128 * k + 128, :] = dot_nt(fluid[k].reshape(128, NZ).astype(BF16), onehot_z[...])
+        for a in range(CX):
+            sample(CX * k + a)
     for j in range(2):
         for h in range(2):
             backbuf[:, 2 * j + h, :] = samples[j, 128 * h : 128 * h + 128, :].T

time: 41.3 us -> 39.5 us (0.956)
  Pallas kernels: 40.5 us -> 38.7 us
    pallas_call x1, Pallas kernels: 39.2 us -> 37.4 us  [body(): pl.pallas_call(kernel, out_shape=(jax.ShapeDtypeStruct((19, CX, CY, NZ),...]
where the time goes in v4:
time: 39.5 us; the launch traced here: 39.3 us
  Pallas kernels  38.7 us (98%)
  between operations  0.64 us (2%)
    pallas_call x1, Pallas kernels, body(): pl.pallas_call(kernel, out_shape=(jax.ShapeDtypeStruct((19, CX, CY, NZ),...  37.4 us
    pallas_call x1, Pallas kernels, body(): pl.pallas_call(finish, out_shape=(jax.ShapeDtypeStruct((19, CX, CY, NZ),...  1.31 us

profile of v4, /device:TPU:1, one launch (start us, length us, event | category | flops | bytes accessed | tf_op | source)
XLA Modules:
  0.0 39.3 jit_solution(13591581279158676852)
XLA Ops:
  0.6 37.4 %shard_map.85 = (f32[19,4,32,128]{3,2,1,0:T(8,128)S(1)}, f32[128,4,128]{2,1,0:T(4,128)S(1)}, bf16[3072,128]{1,0:T(8,128)(2,1)S(1)}, bf16[48,256]{1,0:T(8,128)(2,1)S(1)}, f32[48,4]{1,0:T(8,128)S(1)}) custom-call(f32[19,4,32,128]{3,2,1,0:T(8,128)} %pop_hbm.1, bf16[3072,128]{1,0:T(8,128)(2,1)} %bitcast.6, bf16[3,48,128]{2,1,0:T(8,128)(2,1)} %bitcast.7, ...), custom_call_target="tpu_custom_call" | custom-call | tf_op jit(solution)/shard_map/pallas_call | solution.py:447
  38.0 1.3 %shard_map.86 = (f32[19,4,32,128]{3,2,1,0:T(8,128)}, f32[3,48,128]{2,1,0:T(8,128)}, f32[3,4]{1,0:T(4,128)}) custom-call(f32[19,4,32,128]{3,2,1,0:T(8,128)S(1)} %get-tuple-element.11.fields, f32[128,4,128]{2,1,0:T(4,128)S(1)} %get-tuple-element.12.finbuf, bf16[3072,128]{1,0:T(8,128)(2,1)S(1)} %get-tuple-element.13.weights, ...), custom_call_target="tpu_custom_call" | custom-call | tf_op jit(solution)/shard_map/pallas_call | solution.py:493

commit v5 on v4

--- a/solution.py
+++ b/solution.py
@@ -95,7 +95,7 @@
     pop_hbm, weights_hbm, force_hbm, owner_hbm, base_hbm, swimmer_hbm,
     new_pop, finbuf, weights, take_out, member_out,
     pop, force, owner, base, swimmer,
-    sendbuf, recvbuf, backbuf, turned, spread_hi, spread_lo, onehot_z, forcing, pad1, pad2, fluid, sampled, samples,
+    sendbuf, recvbuf, backbuf, turned, spread, onehot_z, forcing, pad1, pad2, fluid, sampled, samples,
     ysend, yrecv, csend, crecv,
     load_sem, send_sem, recv_sem, halo_send, halo_recv,
 ):
@@ -112,8 +112,10 @@
 
     along_x = [lax.rem(my_x + d, 4) * 2 for d in (1, 3, 2, 0)]
 
-    def to_all(act):
+    def to_all(act, far=False):
         def offset(digit):
+            if far:
+                return jnp.where(digit < 2, 2 - digit, lax.rem(digit + 1, 4))
             return jnp.where(digit < 2, 2 * digit + 1, 6 - 2 * digit)
 
         def step(i, _):
@@ -133,7 +135,7 @@
         act(gx + 1 - 2 * core, gy)
 
     barrier = pltpu.get_barrier_semaphore()
-    to_all(lambda tx, ty: pl.semaphore_signal(barrier, inc=1, device_id=(tx, ty), device_id_type=MESH))
+    to_all(lambda tx, ty: pl.semaphore_signal(barrier, inc=1, device_id=(tx, ty), device_id_type=MESH), far=True)
 
     for load in loads:
         load.start()
@@ -225,8 +227,8 @@
         offs = [sub + 8 * v - y_first for v in range(4)]
         inside.append([(off >= 0) & (off < 4) for off in offs])
 
-    def place(ka):
-        rows = slice(32 * ka, 32 * ka + 32)
+    def place(k, a):
+        ka = CX * k + a
         for c in range(4):
             for j in range(2):
                 x = turned[j, pl.ds(ka * 16 + c, 8, stride=4), :]
@@ -235,16 +237,16 @@
                 hi = x.astype(BF16).astype(F32)
                 lo = x - hi
                 start = 256 * c + 128 * j
-                for piece, ref in ((hi, spread_hi), (lo, spread_lo)):
-                    ref[rows, start : start + 128] = jnp.concatenate(
+                for piece, rows in ((hi, slice(32 * a, 32 * a + 32)), (lo, slice(128 + 32 * a, 160 + 32 * a))):
+                    spread[k, rows, start : start + 128] = jnp.concatenate(
                         [jnp.where(inside[j][v], piece, 0.0) for v in range(4)], axis=0
                     ).astype(BF16)
 
     for k in range(3):
         for a in range(CX):
-            place(CX * k + a)
-        rows = slice(128 * k, 128 * k + 128)
-        forcing[k] = (dot(spread_hi[rows, :], onehot_z[...]) + dot(spread_lo[rows, :], onehot_z[...])).reshape(CX, CY, NZ)
+            place(k, a)
+        both = dot(spread[k], onehot_z[...])
+        forcing[k] = (both[:128] + both[128:]).reshape(CX, CY, NZ)
 
     east, west = (lax.rem(gx + 1, NGX), gy), (lax.rem(gx + NGX - 1, NGX), gy)
     up, down_ = lax.rem(gy + 1, NGY), lax.rem(gy + NGY - 1, NGY)
@@ -277,28 +279,36 @@
         for d in range(19):
             pad[AT[d], x + 1, TOP + 8 * yc : TOP + 8 * yc + 8, :] = out[d]
 
-    def halo_start(pad, n):
-        def copy(source, target, i, device):
-            c = pltpu.make_async_remote_copy(
-                source, target, halo_send.at[n, i], halo_recv.at[n, i], device_id=device, device_id_type=MESH
-            )
-            c.start()
-            return c
-
-        rows = pl.ds(TOP, CY)
+    def halo_copy(source, target, n, i, device):
+        c = pltpu.make_async_remote_copy(
+            source, target, halo_send.at[n, i], halo_recv.at[n, i], device_id=device, device_id_type=MESH
+        )
+        c.start()
+        return c
+
+    def send_corners(pad, n):
         copies = []
         for i, (d, device) in enumerate(corners):
             x = CX if VEL[d][0] == 1 else 1
             y = TOP + CY - 1 if VEL[d][1] == 1 else TOP
             csend[n, i] = pad[AT[d], x, y : y + 1, :]
-            copies.append(copy(csend.at[n, i], crecv.at[n, i], 4 + i, device))
-        copies.append(copy(pad.at[0:5, CX, rows, :], pad.at[0:5, 0, rows, :], 0, east))
-        copies.append(copy(pad.at[5:10, 1, rows, :], pad.at[5:10, CX + 1, rows, :], 1, west))
+            copies.append(halo_copy(csend.at[n, i], crecv.at[n, i], n, 4 + i, device))
+        return copies
+
+    def send_x(pad, n):
+        rows = pl.ds(TOP, CY)
+        return [
+            halo_copy(pad.at[0:5, CX, rows, :], pad.at[0:5, 0, rows, :], n, 0, east),
+            halo_copy(pad.at[5:10, 1, rows, :], pad.at[5:10, CX + 1, rows, :], n, 1, west),
+        ]
+
+    def send_y(pad, n):
+        copies = []
         for side, dirs, edge, device in ((0, YP, TOP + CY - 1, north), (1, YM, TOP, south)):
             for i, d in enumerate(dirs):
                 for x in range(CX):
                     ysend[n, side, i, x : x + 1, :] = pad[AT[d], x + 1, edge : edge + 1, :]
-            copies.append(copy(ysend.at[n, side], yrecv.at[n, side], 2 + side, device))
+            copies.append(halo_copy(ysend.at[n, side], yrecv.at[n, side], n, 2 + side, device))
         return copies
 
     def halo_finish(pad, n, copies):
@@ -313,27 +323,20 @@
             y = TOP - 1 if VEL[d][1] == 1 else TOP + CY
             pad[AT[d], x, y : y + 1, :] = crecv[n, i]
 
-    def rim(work):
-        def sides(i, _):
-            for yc in range(4):
-                work(i * (CX - 1), yc)
-            return 0
-
-        def middle(x, _):
-            work(x, 0)
-            work(x, 3)
-            return 0
-
-        lax.fori_loop(0, 2, sides, 0)
-        lax.fori_loop(1, CX - 1, middle, 0)
-
-    def core_cells(work):
-        def middle(x, _):
-            work(x, 1)
-            work(x, 2)
-            return 0
-
-        lax.fori_loop(1, CX - 1, middle, 0)
+    def cells(work, xs, ycs):
+        for x in xs:
+            for yc in ycs:
+                work(x, yc)
+
+    outer, inner = (0, 3), (1, 2)
+
+    def rim_sent(work, pad, n):
+        cells(work, outer, outer)
+        copies = send_corners(pad, n)
+        cells(work, outer, inner)
+        copies += send_x(pad, n)
+        cells(work, inner, outer)
+        return copies + send_y(pad, n)
 
     def step1(x, yc):
         collided(pad1, [pop[d, x, 8 * yc : 8 * yc + 8, :] for d in range(19)], x, yc)
@@ -342,26 +345,27 @@
         collided(pad2, [pulled(pad1, d, x, yc) for d in range(19)], x, yc)
 
     def step3(x, yc):
-        f = [pulled(pad2, d, x, yc) for d in range(19)]
         at = slice(8 * yc, 8 * yc + 8)
-        for d in range(19):
-            new_pop[d, x, at, :] = f[d]
-        rho, mom = moments(f)
+        rho, mom = moments([pulled(pad2, d, x, yc) for d in range(19)])
         inv = 1.0 / rho
         for k in range(3):
             fluid[k, x, at, :] = (mom[k] + 0.5 * forcing[k, x, at, :]) * inv
 
+    def keep(x, yc):
+        for d in range(19):
+            new_pop[d, x, 8 * yc : 8 * yc + 8, :] = pulled(pad2, d, x, yc)
+
+    every = range(4)
     loads[5].wait()
-    rim(step1)
-    halo1 = halo_start(pad1, 0)
-    core_cells(step1)
-    core_cells(step2)
+    halo1 = rim_sent(step1, pad1, 0)
+    cells(step1, inner, inner)
+    cells(step2, inner, inner)
     halo_finish(pad1, 0, halo1)
-    rim(step2)
-    halo2 = halo_start(pad2, 1)
-    core_cells(step3)
+    halo2 = rim_sent(step2, pad2, 1)
+    cells(step3, inner, inner)
     halo_finish(pad2, 1, halo2)
-    rim(step3)
+    cells(step3, outer, every)
+    cells(step3, inner, outer)
 
     for j in range(2):
         samples[j, 192:256, :] = jnp.zeros((64, 128), F32)
@@ -385,6 +389,7 @@
         for h in range(2):
             backbuf[:, 2 * j + h, :] = samples[j, 128 * h : 128 * h + 128, :].T
     exchange(backbuf, finbuf, 1)
+    lax.fori_loop(0, CX, lambda x, c: (cells(keep, (x,), every), c)[1], 0)
     exchanged(backbuf, finbuf, 1).wait_recv()
 
     exchanged(sendbuf, recvbuf, 0).wait_send()
@@ -465,8 +470,7 @@
             pltpu.VMEM((NDEV, 4, 128), F32),
             pltpu.VMEM((NDEV, 4, 128), F32),
             pltpu.VMEM((2, 256, 128), F32),
-            pltpu.VMEM((384, 1024), BF16),
-            pltpu.VMEM((384, 1024), BF16),
+            pltpu.VMEM((3, 256, 1024), BF16),
             pltpu.VMEM((1024, 128), BF16),
             pltpu.VMEM((3, CX, CY, NZ), F32),
             pltpu.VMEM((19, CX + 2, CY + 16, NZ), F32),

time: 39.5 us -> 38.4 us (0.972)
  Pallas kernels: 38.7 us -> 37.7 us
    pallas_call x1, Pallas kernels: 37.4 us -> 36.3 us  [body(): pl.pallas_call(kernel, out_shape=(jax.ShapeDtypeStruct((19, CX, CY, NZ),...]
where the time goes in v5:
time: 38.4 us; the launch traced here: 38.3 us
  Pallas kernels  37.7 us (98%)
  between operations  0.64 us (2%)
    pallas_call x1, Pallas kernels, body(): pl.pallas_call(kernel, out_shape=(jax.ShapeDtypeStruct((19, CX, CY, NZ),...  36.3 us
    pallas_call x1, Pallas kernels, body(): pl.pallas_call(finish, out_shape=(jax.ShapeDtypeStruct((19, CX, CY, NZ),...  1.32 us

profile of v5, /device:TPU:1, one launch (start us, length us, event | category | flops | bytes accessed | tf_op | source)
XLA Modules:
  0.0 38.3 jit_solution(1494144405758570676)
XLA Ops:
  0.6 36.3 %shard_map.85 = (f32[19,4,32,128]{3,2,1,0:T(8,128)S(1)}, f32[128,4,128]{2,1,0:T(4,128)S(1)}, bf16[3072,128]{1,0:T(8,128)(2,1)S(1)}, bf16[48,256]{1,0:T(8,128)(2,1)S(1)}, f32[48,4]{1,0:T(8,128)S(1)}) custom-call(f32[19,4,32,128]{3,2,1,0:T(8,128)} %pop_hbm.1, bf16[3072,128]{1,0:T(8,128)(2,1)} %bitcast.6, bf16[3,48,128]{2,1,0:T(8,128)(2,1)} %bitcast.7, ...), custom_call_target="tpu_custom_call" | custom-call | tf_op jit(solution)/shard_map/pallas_call | solution.py:452
  37.0 1.3 %shard_map.86 = (f32[19,4,32,128]{3,2,1,0:T(8,128)}, f32[3,48,128]{2,1,0:T(8,128)}, f32[3,4]{1,0:T(4,128)}) custom-call(f32[19,4,32,128]{3,2,1,0:T(8,128)S(1)} %get-tuple-element.11.fields, f32[128,4,128]{2,1,0:T(4,128)S(1)} %get-tuple-element.12.finbuf, bf16[3072,128]{1,0:T(8,128)(2,1)S(1)} %get-tuple-element.13.weights, ...), custom_call_target="tpu_custom_call" | custom-call | tf_op jit(solution)/shard_map/pallas_call | solution.py:497

commit v6 on v5

--- a/solution.py
+++ b/solution.py
@@ -112,11 +112,9 @@
 
     along_x = [lax.rem(my_x + d, 4) * 2 for d in (1, 3, 2, 0)]
 
-    def to_all(act, far=False):
+    def to_all(act):
         def offset(digit):
-            if far:
-                return jnp.where(digit < 2, 2 - digit, lax.rem(digit + 1, 4))
-            return jnp.where(digit < 2, 2 * digit + 1, 6 - 2 * digit)
+            return jnp.where(digit < 2, 2 - digit, lax.rem(digit + 1, 4))
 
         def step(i, _):
             z = lax.rem(my_z + offset(lax.div(i, 4)), 4)
@@ -135,7 +133,7 @@
         act(gx + 1 - 2 * core, gy)
 
     barrier = pltpu.get_barrier_semaphore()
-    to_all(lambda tx, ty: pl.semaphore_signal(barrier, inc=1, device_id=(tx, ty), device_id_type=MESH), far=True)
+    to_all(lambda tx, ty: pl.semaphore_signal(barrier, inc=1, device_id=(tx, ty), device_id_type=MESH))
 
     for load in loads:
         load.start()

time: 38.4 us -> 37.8 us (0.984)
  Pallas kernels: 37.7 us -> 37 us
    pallas_call x1, Pallas kernels: 36.3 us -> 35.7 us  [body(): pl.pallas_call(kernel, out_shape=(jax.ShapeDtypeStruct((19, CX, CY, NZ),...]
where the time goes in v6:
time: 37.8 us; the launch traced here: 37.7 us
  Pallas kernels  37 us (98%)
  between operations  0.64 us (2%)
    pallas_call x1, Pallas kernels, body(): pl.pallas_call(kernel, out_shape=(jax.ShapeDtypeStruct((19, CX, CY, NZ),...  35.7 us
    pallas_call x1, Pallas kernels, body(): pl.pallas_call(finish, out_shape=(jax.ShapeDtypeStruct((19, CX, CY, NZ),...  1.32 us

profile of v6, /device:TPU:1, one launch (start us, length us, event | category | flops | bytes accessed | tf_op | source)
XLA Modules:
  0.0 37.7 jit_solution(11947695005558603423)
XLA Ops:
  0.6 35.7 %shard_map.85 = (f32[19,4,32,128]{3,2,1,0:T(8,128)S(1)}, f32[128,4,128]{2,1,0:T(4,128)S(1)}, bf16[3072,128]{1,0:T(8,128)(2,1)S(1)}, bf16[48,256]{1,0:T(8,128)(2,1)S(1)}, f32[48,4]{1,0:T(8,128)S(1)}) custom-call(f32[19,4,32,128]{3,2,1,0:T(8,128)} %pop_hbm.1, bf16[3072,128]{1,0:T(8,128)(2,1)} %bitcast.6, bf16[3,48,128]{2,1,0:T(8,128)(2,1)} %bitcast.7, ...), custom_call_target="tpu_custom_call" | custom-call | tf_op jit(solution)/shard_map/pallas_call | solution.py:450
  36.4 1.3 %shard_map.86 = (f32[19,4,32,128]{3,2,1,0:T(8,128)}, f32[3,48,128]{2,1,0:T(8,128)}, f32[3,4]{1,0:T(4,128)}) custom-call(f32[19,4,32,128]{3,2,1,0:T(8,128)S(1)} %get-tuple-element.11.fields, f32[128,4,128]{2,1,0:T(4,128)S(1)} %get-tuple-element.12.finbuf, bf16[3072,128]{1,0:T(8,128)(2,1)S(1)} %get-tuple-element.13.weights, ...), custom_call_target="tpu_custom_call" | custom-call | tf_op jit(solution)/shard_map/pallas_call | solution.py:495

commit v7 on v6

--- a/solution.py
+++ b/solution.py
@@ -188,18 +188,18 @@
 
     pl.semaphore_wait(barrier, NDEV - 1)
 
-    def exchange(source, target, n):
+    def exchange(source, target, n, rows=4):
         to_all(
             lambda tx, ty: pltpu.make_async_remote_copy(
-                source.at[tx * NGY + ty], target.at[me], send_sem.at[n], recv_sem.at[n],
+                source.at[tx * NGY + ty, 0:rows], target.at[me, 0:rows], send_sem.at[n], recv_sem.at[n],
                 device_id=(tx, ty), device_id_type=MESH,
             ).start()
         )
-        target[me] = source[me]
-
-    def exchanged(source, target, n):
+        target[me, 0:rows] = source[me, 0:rows]
+
+    def exchanged(source, target, n, rows=4):
         return pltpu.make_async_remote_copy(
-            source.at[pl.ds(0, NDEV - 1)], target.at[pl.ds(0, NDEV - 1)], send_sem.at[n], recv_sem.at[n],
+            source.at[pl.ds(0, NDEV - 1), 0:rows], target.at[pl.ds(0, NDEV - 1), 0:rows], send_sem.at[n], recv_sem.at[n],
             device_id=(lax.rem(gx + 1, NGX), gy), device_id_type=MESH,
         )
 
@@ -365,9 +365,6 @@
     cells(step3, outer, every)
     cells(step3, inner, outer)
 
-    for j in range(2):
-        samples[j, 192:256, :] = jnp.zeros((64, 128), F32)
-
     def sample(ka):
         for c in range(4):
             for j in range(2):
@@ -384,14 +381,14 @@
         for a in range(CX):
             sample(CX * k + a)
     for j in range(2):
-        for h in range(2):
-            backbuf[:, 2 * j + h, :] = samples[j, 128 * h : 128 * h + 128, :].T
-    exchange(backbuf, finbuf, 1)
+        backbuf[:, j, :] = samples[j, 0:128, :].T
+    backbuf[:, 2, :] = jnp.concatenate([samples[j, 128:192, :] for j in range(2)], axis=0).T
+    exchange(backbuf, finbuf, 1, 3)
     lax.fori_loop(0, CX, lambda x, c: (cells(keep, (x,), every), c)[1], 0)
-    exchanged(backbuf, finbuf, 1).wait_recv()
+    exchanged(backbuf, finbuf, 1, 3).wait_recv()
 
     exchanged(sendbuf, recvbuf, 0).wait_send()
-    exchanged(backbuf, finbuf, 1).wait_send()
+    exchanged(backbuf, finbuf, 1, 3).wait_send()
     for c in halo1 + halo2:
         c.wait_send()
 
@@ -408,8 +405,13 @@
     stores[0].start()
     left = iota((8, 128), 1) < 64
     ownpart = own_part()
+    thirds = finbuf[:, 2, :]
     back = jnp.concatenate(
-        [jnp.concatenate([finbuf[:, 2 * j + h, :] for h in range(2)], axis=1) for j in range(2)], axis=0
+        [
+            jnp.concatenate([finbuf[:, 0, :], thirds], axis=1),
+            jnp.concatenate([finbuf[:, 1, :], pltpu.roll(thirds, 64, 1)], axis=1),
+        ],
+        axis=0,
     ).astype(BF16)
     cells = dot(take[...], back)
     means = [[], [], []]

time: 37.8 us -> 37.4 us (0.989)
  no operation moved by 1% of the time
where the time goes in v7:
time: 37.4 us; the launch traced here: 37.3 us
  Pallas kernels  36.7 us (98%)
  between operations  0.64 us (2%)
    pallas_call x1, Pallas kernels, body(): pl.pallas_call(kernel, out_shape=(jax.ShapeDtypeStruct((19, CX, CY, NZ),...  35.4 us
    pallas_call x1, Pallas kernels, body(): pl.pallas_call(finish, out_shape=(jax.ShapeDtypeStruct((19, CX, CY, NZ),...  1.29 us

profile of v7, /device:TPU:1, one launch (start us, length us, event | category | flops | bytes accessed | tf_op | source)
XLA Modules:
  0.0 37.3 jit_solution(12780095636504829831)
XLA Ops:
  0.6 35.4 %shard_map.85 = (f32[19,4,32,128]{3,2,1,0:T(8,128)S(1)}, f32[128,4,128]{2,1,0:T(4,128)S(1)}, bf16[3072,128]{1,0:T(8,128)(2,1)S(1)}, bf16[48,256]{1,0:T(8,128)(2,1)S(1)}, f32[48,4]{1,0:T(8,128)S(1)}) custom-call(f32[19,4,32,128]{3,2,1,0:T(8,128)} %pop_hbm.1, bf16[3072,128]{1,0:T(8,128)(2,1)} %bitcast.6, bf16[3,48,128]{2,1,0:T(8,128)(2,1)} %bitcast.7, ...), custom_call_target="tpu_custom_call" | custom-call | tf_op jit(solution)/shard_map/pallas_call | solution.py:452
  36.0 1.3 %shard_map.86 = (f32[19,4,32,128]{3,2,1,0:T(8,128)}, f32[3,48,128]{2,1,0:T(8,128)}, f32[3,4]{1,0:T(4,128)}) custom-call(f32[19,4,32,128]{3,2,1,0:T(8,128)S(1)} %get-tuple-element.11.fields, f32[128,4,128]{2,1,0:T(4,128)S(1)} %get-tuple-element.12.finbuf, bf16[3072,128]{1,0:T(8,128)(2,1)S(1)} %get-tuple-element.13.weights, ...), custom_call_target="tpu_custom_call" | custom-call | tf_op jit(solution)/shard_map/pallas_call | solution.py:497
